TPU v7x, 32 devices: a whole 2x2x4 slice. The times are simulated.
32 devices in a mesh: row: 4 (over z), col: 8 (over y, x, core).
Axes of the slice: x: 2, y: 2, z: 4, core: 2. Of those that a mesh axis runs over, the one named last changes fastest.
Arguments:
- front: float32 [16384, 16384], P('row', 'col')
- tiles: float32 [4096, 128, 128], P(('row', 'col')), may hold values from -0.375 to 0.375
- tile_block: int32 [2, 4096], replicated, may hold values from 0 to 127, as said below
- valid_rows: int32 [4096], P(('row', 'col')), may hold values from 64 to 128
Outputs:
- factored: float32 [16384, 16384], P('row', 'col')
Inputs may be any that keep to these rules, and one draw needn't show every extreme that they name: tile_block[0, t] and tile_block[1, t] give the block row and block column, in blocks of 128, that tile t is added to. The 128 tiles of each device (tiles laid in order over row+col) go to blocks held by exactly 16 different devices, 8 tiles to each.
All inputs are finite; a program needn't handle non-finite values.
Results may differ from a plain program's by a relative error of at most 0.0001.
Values sent between devices are 32-bit elements; how exact they have to be, the bound alone decides.
No kernel may reach another device: no remote copies, remote signals or barrier semaphores. Data moves between devices by JAX's collectives and lax.ppermute only.
A program may use at most 192 MiB of HBM per device.

v0:
```python
import jax
import jax.numpy as jnp
from jax import lax
from jax.sharding import PartitionSpec as P

NB = 128
PANELS = 2


precise = lax.Precision.HIGHEST


def broadcast(value, axis, source):
    kept = jnp.where(lax.axis_index(axis) == source, value, 0).astype(value.dtype)
    return lax.psum(kept, axis)


def factor_panel(current, offset, row_now, col_now, global_row):
    row_len = current.shape[0]
    ending = offset + NB
    diagonal = current[offset:ending, offset:ending]
    symmetric = jnp.tril(diagonal) + jnp.tril(diagonal, -1).T
    is_owner = (row_now == 0) & (col_now == 0)
    symmetric = jnp.where(is_owner, symmetric, jnp.eye(NB, dtype=jnp.float32))
    lower = jnp.linalg.cholesky(symmetric)
    lower = broadcast(lower, "row", 0)
    solved = jax.scipy.linalg.solve_triangular(lower, current[:, offset:ending].T, lower=True).T
    placed = jnp.zeros((row_len, NB), jnp.float32).at[offset:ending].set(lower)
    return jnp.where(global_row < offset, 0.0, jnp.where(global_row < ending, placed, solved))


def body(front, tiles, tile_block, valid_rows):
    row_len, col_len = front.shape
    row_count = lax.axis_size("row")
    col_count = lax.axis_size("col")
    device_count = row_count * col_count
    per_device = tiles.shape[0]
    tile_side = tiles.shape[1]
    capacity = 2 * per_device // device_count
    rows_blocks = row_len // tile_side
    cols_blocks = col_len // tile_side
    row_now = lax.axis_index("row")
    col_now = lax.axis_index("col")
    device_now = row_now * col_count + col_now
    target = tile_block[0] // rows_blocks * col_count + tile_block[1] // cols_blocks
    grouped = target.reshape(device_count, per_device)
    positions = jnp.arange(per_device)
    earlier = positions[None, :] < positions[:, None]
    same_target = grouped[:, :, None] == grouped[:, None, :]
    ranking = jnp.sum(same_target & earlier[None], axis=2)
    own_target = lax.dynamic_index_in_dim(grouped, device_now, 0, keepdims=False)
    own_rank = lax.dynamic_index_in_dim(ranking, device_now, 0, keepdims=False)
    keeping = jnp.arange(tile_side)[None, :, None] < valid_rows[:, None, None]
    masked = jnp.where(keeping, tiles, 0.0)
    outgoing = jnp.zeros((device_count * capacity, tile_side, tile_side), jnp.float32)
    outgoing = outgoing.at[own_target * capacity + own_rank].set(masked)
    arrived = lax.all_to_all(
        outgoing.reshape(device_count, capacity, tile_side, tile_side),
        ("row", "col"),
        split_axis=0,
        concat_axis=0,
        tiled=True,
    )
    arrived = arrived.reshape(device_count * capacity, tile_side, tile_side)
    source = (jnp.arange(device_count * per_device) // per_device).reshape(device_count, per_device)
    slot_in = jnp.where(
        grouped == device_now, source * capacity + ranking, device_count * capacity
    ).reshape(-1)
    slot_row = (
        jnp.zeros((device_count * capacity,), jnp.int32)
        .at[slot_in]
        .set(tile_block[0] % rows_blocks, mode="drop")
    )
    slot_col = (
        jnp.zeros((device_count * capacity,), jnp.int32)
        .at[slot_in]
        .set(tile_block[1] % cols_blocks, mode="drop")
    )
    blocked = front.reshape(rows_blocks, tile_side, cols_blocks, tile_side)
    blocked = blocked.at[slot_row, :, slot_col, :].add(arrived)
    current = blocked.reshape(row_len, col_len)
    total = PANELS * NB
    global_row = row_now * row_len + jnp.arange(row_len)[:, None]
    global_col = col_now * col_len + jnp.arange(col_len)[None, :]
    slice_start = col_now * col_len % row_len
    slice_root = col_now * col_len // row_len
    stacked_parts = []
    for number in range(PANELS):
        offset = number * NB
        panel_here = factor_panel(current, offset, row_now, col_now, global_row)
        stacked_parts.append(panel_here)
        if number + 1 < PANELS:
            later = broadcast(panel_here[offset + NB : total], "row", 0)
            change = jnp.dot(
                panel_here, later.T, precision=precise, preferred_element_type=jnp.float32
            )
            columns = current[:, offset + NB : total]
            inside = (global_row >= offset + NB) & (col_now == 0)
            current = current.at[:, offset + NB : total].set(
                jnp.where(inside, columns - change, columns)
            )
    stacked = jnp.concatenate(stacked_parts, 1)
    rows_all = broadcast(stacked, "col", 0)
    cols_all = broadcast(
        lax.dynamic_slice_in_dim(rows_all, slice_start, col_len, 0), "row", slice_root
    )
    change = jnp.dot(rows_all, cols_all.T, precision=precise, preferred_element_type=jnp.float32)
    inside = (global_row >= total) & (global_col >= total)
    current = jnp.where(inside, current - change, current)
    left_part = jnp.concatenate([rows_all, jnp.zeros((row_len, col_len - total), jnp.float32)], 1)
    upper_part = jnp.concatenate(
        [cols_all.T, jnp.zeros((row_len - total, col_len), jnp.float32)], 0
    )
    upper_mask = (global_row < total) & (global_col >= total)
    return jnp.where(global_col < total, left_part, jnp.where(upper_mask, upper_part, current))


def solution(mesh):
    placed = (P("row", "col"), P(("row", "col"), None, None), P(), P(("row", "col")))
    return jax.shard_map(
        body, mesh=mesh, in_specs=placed, out_specs=P("row", "col"), check_vma=False
    )
```

profile of v0, /device:TPU:7, one launch (start us, length us, event | category | flops | bytes accessed | tf_op | source)
XLA Modules:
  0.0 988.4 jit_solution(14368992151038991531)
XLA Ops:
  9.5 9.9 %broadcast_select_fusion = f32[128,128,128]{2,1,0:T(8,128)} fusion(f32[128,128,128]{2,1,0:T(8,128)} %param.14, pred[128,128]{1,0:T(8,128)(4,1)S(1)} %iota_compare_fusion.5), kind=kLoop, calls=%fused_computation.18 | loop fusion | flops 2097152 | bytes 16793600 | tf_op jit(solution)/shard_map/jit(_where)/select_n | solution.py:54
  19.4 7.8 broadcast_in_dim.109
  27.3 23.4 %scatter_fusion = f32[256,128,128]{2,1,0:T(8,128)} fusion(f32[256,128,128]{2,1,0:T(8,128)} %broadcast_in_dim.109, s32[128]{0:T(128)S(1)} %fusion.34, f32[128,128,128]{2,1,0:T(8,128)} %broadcast_select_fusion), kind=kCustom, calls=%fused_computation.2 | custom fusion | bytes 25166336 | tf_op jit(solution)/shard_map/scatter | solution.py:56
  50.7 6.4 all-to-all-start
  57.4 15.5 %scatter_custom_fusion = s32[256]{0:T(256)S(1)} fusion(s32[4096]{0:T(1024)S(1)} %bitcast.109, s32[4096]{0:T(1024)S(1)} %add_select_fusion.1, s32[]{:T(128)} %constant.228.clone.1), kind=kCustom, calls=%fused_computation.115 | custom fusion | bytes 1028 | tf_op jit(solution)/shard_map/scatter | solution.py:72
  73.0 15.7 %scatter_custom_fusion.1 = s32[256]{0:T(256)S(1)} fusion(s32[4096]{0:T(1024)S(1)} %bitcast.110, s32[4096]{0:T(1024)S(1)} %add_select_fusion, s32[]{:T(128)} %constant.228.clone.1), kind=kCustom, calls=%fused_computation.113 | custom fusion | bytes 1028 | tf_op jit(solution)/shard_map/scatter | solution.py:77
  88.7 17.2 %copy.79 = f32[512,8,16,128]{3,2,1,0:T(8,128)S(1)} copy(f32[512,8,16,128]{3,1,2,0:T(8,128)} %bitcast.102) | data formatting | bytes 67108864
  105.9 14.6 %copy.48 = f32[32,128,16,128]{3,1,2,0:T(8,128)} copy(f32[32,128,16,128]{3,2,1,0:T(8,128)S(1)} %bitcast.95) | data formatting | bytes 67108864 | tf_op jit(solution)/shard_map/reshape | solution.py:79
  121.2 301.0 %all-to-all-done = f32[32,8,128,128]{3,2,1,0:T(8,128)} async-done(((f32[32,8,128,128]{3,2,1,0:T(8,128)}), f32[32,8,128,128]{3,2,1,0:T(8,128)}, u32[]{:S(2)}, u32[]{:S(2)}) %all-to-all-start) | async-done | bytes 16777248 | tf_op jit(solution)/shard_map/all_to_all | solution.py:57
  422.3 54.5 %scatter_fusion.1 = f32[32,128,16,128]{3,1,2,0:T(8,128)} fusion(f32[32,128,16,128]{3,1,2,0:T(8,128)} %copy.48, s32[256]{0:T(256)S(1)} %bitcast.103, f32[256,128,128]{2,1,0:T(8,128)} %bitcast.14), kind=kCustom, calls=%fused_computation.3 | custom fusion | flops 4194304 | bytes 50333696 | tf_op jit(solution)/shard_map/scatter-add | solution.py:80
  476.7 34.6 %copy.49 = f32[32,128,16,128]{1,0,3,2:T(8,128)} copy(f32[32,128,16,128]{3,1,2,0:T(8,128)} %scatter_fusion.1) | data formatting | bytes 67108864 | tf_op jit(solution)/shard_map/scatter-add | solution.py:80
  511.3 36.4 %copy.82 = f32[256,8,32,128]{3,1,2,0:T(8,128)S(1)} copy(f32[256,8,32,128]{3,2,1,0:T(8,128)} %bitcast.94) | data formatting | bytes 67108864
  547.7 11.7 %copy-done = f32[256,8,32,128]{3,1,2,0:T(8,128)} copy-done((f32[256,8,32,128]{3,1,2,0:T(8,128)}, f32[256,8,32,128]{3,1,2,0:T(8,128)S(1)}, u32[]{:S(2)}) %copy-start) | copy-done | bytes 33554456
  560.6 11.7 %cholesky.44 = f32[128,128]{1,0:T(8,128)S(1)} custom-call(f32[128,128]{1,0:T(8,128)S(1)} %copy.52), custom_call_target="Cholesky" | custom-call | tf_op jit(solution)/shard_map/jit(cholesky)/cholesky | solution.py:25
  574.5 34.4 %all-reduce.10.cloned.1.call-done = f32[128,128]{0,1:T(8,128)} async-done(((f32[128,128]{0,1:T(8,128)}), f32[128,128]{0,1:T(8,128)}) %all-reduce.10.cloned.1.call-update) | async-done | bytes 65552 | tf_op jit(solution)/shard_map/psum | solution.py:15
  609.8 9.8 custom-call.8
  619.7 3.6 fusion.7
  625.8 33.3 %all-reduce.12.cloned.1.call-done = f32[128,128]{0,1:T(8,128)} async-done(((f32[128,128]{0,1:T(8,128)}), f32[128,128]{0,1:T(8,128)}) %all-reduce.12.cloned.1.call-update) | async-done | bytes 65552 | tf_op jit(solution)/shard_map/psum | solution.py:15
  659.1 5.0 fusion.5
  664.5 11.7 %cholesky.55 = f32[128,128]{1,0:T(8,128)S(1)} custom-call(f32[128,128]{1,0:T(8,128)S(1)} %copy.59), custom_call_target="Cholesky" | custom-call | tf_op jit(solution)/shard_map/jit(cholesky)/cholesky | solution.py:25
  678.7 2.9 copy.66
  681.6 30.7 %all-reduce.14.cloned.1.call-done = f32[128,128]{1,0:T(8,128)} async-done(((f32[128,128]{1,0:T(8,128)}), f32[128,128]{1,0:T(8,128)}) %all-reduce.14.cloned.1.call-update) | async-done | bytes 65552 | tf_op jit(solution)/shard_map/psum | solution.py:15
  713.2 9.8 custom-call.9
  723.0 5.4 fusion.3
  728.4 2.2 maximum_select_fusion
  731.0 81.8 %all-reduce.16.cloned.1.call-done = f32[4096,256]{1,0:T(8,128)} async-done(((f32[4096,256]{1,0:T(8,128)}), f32[4096,256]{1,0:T(8,128)}) %all-reduce.16.cloned.1.call-update) | async-done | bytes 4194320 | tf_op jit(solution)/shard_map/psum | solution.py:15
  812.7 3.1 dynamic-slice_select_fusion
  815.9 1.5 constant_dynamic-update-slice_fusion
  817.3 5.6 copy.67
  823.0 80.4 %all-reduce.18.cloned.1.call-done = f32[2048,256]{1,0:T(8,128)} async-done(((f32[2048,256]{1,0:T(8,128)}), f32[2048,256]{1,0:T(8,128)}) %all-reduce.18.cloned.1.call-update) | async-done | bytes 2097168 | tf_op jit(solution)/shard_map/psum | solution.py:15
  903.3 45.0 %fusion.1 = f32[4096,2048]{0,1:T(8,128)} fusion(f32[4096,2048]{0,1:T(8,128)} %constant_dynamic-update-slice_fusion, f32[256,2048]{0,1:T(8,128)} %bitcast.113, f32[4096,256]{0,1:T(8,128)} %copy.67, pred[2048]{0:T(1024)(128)(4,1)S(1)} %get-tuple-element.50, pred[4096]{0:T(1024)(128)(4,1)S(1)} %fusion.21, pred[4096]{0:T(1024)(128)(4,1)S(1)} %fusion.23, ...), kind=kOutput, calls=%fused_computation.6 | convolution fusion | flops 25820135424 | bytes 79704064 | tf_op jit(solution)/shard_map/dot_general | solution.py:107
  948.3 33.3 %copy.69 = f32[4096,2048]{1,0:T(8,128)} copy(f32[4096,2048]{0,1:T(8,128)} %fusion.1) | data formatting | bytes 67108864 | tf_op jit(solution)/shard_map/jit(_where)/select_n | solution.py:115
  (60 shorter events, 14.6 us)
Async XLA Ops:
  50.7 6.5 copy-start.3
  50.7 371.6 %all-to-all-start = ((f32[32,8,128,128]{3,2,1,0:T(8,128)}), f32[32,8,128,128]{3,2,1,0:T(8,128)}, u32[]{:S(2)}, u32[]{:S(2)}) async-start(f32[32,8,128,128]{3,2,1,0:T(8,128)} %bitcast.96), calls=%async_computation | async-start | bytes 33554432 | tf_op jit(solution)/shard_map/all_to_all | solution.py:57
  57.1 551.7 %all-reduce.10.cloned.1.call-start = ((), (), s32[]{:S(2)}) async-start(), calls=%async_computation.1 | async-start | bytes 131072 | tf_op jit(solution)/shard_map/psum | solution.py:15
  547.7 11.7 %copy-start = (f32[256,8,32,128]{3,1,2,0:T(8,128)}, f32[256,8,32,128]{3,1,2,0:T(8,128)S(1)}, u32[]{:S(2)}) copy-start(f32[256,8,32,128]{3,1,2,0:T(8,128)S(1)} %copy.82) | copy-start | bytes 100663296
  574.5 84.6 %all-reduce.12.cloned.1.call-start = ((), (), s32[]{:S(2)}) async-start(), calls=%async_computation.2 | async-start | bytes 131072 | tf_op jit(solution)/shard_map/psum | solution.py:15
  623.3 1.4 copy-start.1
  625.3 87.1 %all-reduce.14.cloned.1.call-start = ((), (), s32[]{:S(2)}) async-start(), calls=%async_computation.3 | async-start | bytes 131072 | tf_op jit(solution)/shard_map/psum | solution.py:15
  678.5 134.3 %all-reduce.16.cloned.1.call-start = ((), (), s32[]{:S(2)}) async-start(), calls=%async_computation.4 | async-start | bytes 8388608 | tf_op jit(solution)/shard_map/psum | solution.py:15
  723.0 5.4 copy-start.2
  730.7 172.7 %all-reduce.18.cloned.1.call-start = ((), (), s32[]{:S(2)}) async-start(), calls=%async_computation.5 | async-start | bytes 4194304 | tf_op jit(solution)/shard_map/psum | solution.py:15
Sparse Core Ops, SparseCore 0:
  574.6 34.2 all-reduce.9
  625.4 33.6 all-reduce.11
  678.6 33.6 all-reduce.13
  730.8 81.8 all-reduce.15
  815.9 87.3 all-reduce.17
where the time goes:
time: 997 us; the launch traced here: 988 us
  waiting for transfers between devices  562 us (56%)
  local copies, waits for them, and re-layouts  224 us (22%)
  other arithmetic  122 us (12%)
  matrix products  59 us (6%)
  between operations  13.8 us (1%)
    all_to_all x1, waiting for transfers between devices, body(): lax.all_to_all(outgoing.reshape(device_count, capacity, tile_side, tile_s...  301 us
    psum x5, waiting for transfers between devices, broadcast(): return lax.psum(kept, axis)  261 us
    unnamed x10, local copies, waits for them, and re-layouts  66.7 us
    scatter-add x1, other arithmetic, body(): blocked = blocked.at[slot_row, :, slot_col, :].add(arrived)  54.5 us
    dot_general x1, matrix products, body(): jnp.dot(rows_all, cols_all.T, precision=precise, preferred_element_type=j...  45 us
    scatter-add x1, local copies, waits for them, and re-layouts, body(): blocked = blocked.at[slot_row, :, slot_col, :].add(arrived)  34.6 us
    select_n x1, local copies, waits for them, and re-layouts, body(): jnp.where(global_col < total, left_part, jnp.where(upper_mask, upper_part...  33.3 us
    another operation x6, other arithmetic, factor_panel(): lower = jnp.linalg.cholesky(symmetric)  25 us
  transfers between devices with their start and end apart: 6, of which 6 were waited for; matrix products, arithmetic and copies ran while one was open for 7% of the time, Pallas kernels for 0%

commit v1 on v0

v1 whole, which is shorter than its diff:
```python
import functools

import jax
import jax.numpy as jnp
from jax import lax
from jax.experimental import pallas as pl
from jax.experimental.pallas import tpu as pltpu
from jax.sharding import PartitionSpec as P

NB = 128
PANELS = 2
TOTAL = NB * PANELS
MIB = 1 << 20


precise = lax.Precision.HIGHEST


def dot_nt(a, b, precision=precise):
    return lax.dot_general(
        a, b, (((1,), (1,)), ((), ())), precision=precision, preferred_element_type=jnp.float32
    )


def pack_kernel(slot_ref, valid_ref, tiles_ref, out_ref, buf, sem_in, sem_out):
    count, side = tiles_ref.shape[0], tiles_ref.shape[1]

    def fetch(t):
        return pltpu.make_async_copy(tiles_ref.at[t], buf.at[t], sem_in.at[t])

    def store(t):
        return pltpu.make_async_copy(buf.at[t], out_ref.at[jnp.maximum(slot_ref[t], 0)], sem_out.at[t])

    def each(act):
        @pl.loop(0, count)
        def _(t):
            @pl.when(slot_ref[t] >= 0)
            def _():
                act(t)

    def mask(t):
        fetch(t).wait()
        rows = lax.broadcasted_iota(jnp.int32, (side, side), 0)
        buf[t] = jnp.where(rows < valid_ref[t], buf[t], 0.0)
        store(t).start()

    each(lambda t: fetch(t).start())
    each(mask)
    each(lambda t: store(t).wait())


def pack(tiles, slots, valid, n_slots):
    count, side = tiles.shape[0], tiles.shape[1]
    smem = pl.BlockSpec(memory_space=pltpu.SMEM)
    return pl.pallas_call(
        pack_kernel,
        out_shape=jax.ShapeDtypeStruct((n_slots, side, side), jnp.float32),
        in_specs=[smem, smem, pl.BlockSpec(memory_space=pl.ANY)],
        out_specs=pl.BlockSpec(memory_space=pl.ANY),
        scratch_shapes=[
            pltpu.VMEM((count, side, side), jnp.float32),
            pltpu.SemaphoreType.DMA((count,)),
            pltpu.SemaphoreType.DMA((count,)),
        ],
        compiler_params=pltpu.CompilerParams(vmem_limit_bytes=24 * MIB),
    )(slots, valid, tiles)


def panel_kernel(code_ref, first_ref, front_ref, arrived_ref, out_ref):
    side = arrived_ref.shape[1]

    @pl.when(first_ref[0] == 1)
    def _():
        out_ref[...] = front_ref[...]

    @pl.when(first_ref[0] == 0)
    def _():
        out_ref[...] = jnp.zeros_like(out_ref)

    @pl.loop(0, arrived_ref.shape[0])
    def _(k):
        code = code_ref[k]
        for part in range(PANELS):

            @pl.when((code >= 0) & (code % PANELS == part))
            def _():
                rows = pl.ds(pl.multiple_of(code // PANELS * side, side), side)
                out_ref[rows, part * side : (part + 1) * side] += arrived_ref[k]


def raw_panel(front, arrived, codes, first):
    row_len = front.shape[0]
    smem = pl.BlockSpec(memory_space=pltpu.SMEM)
    return pl.pallas_call(
        panel_kernel,
        grid=(1,),
        out_shape=jax.ShapeDtypeStruct((row_len, TOTAL), jnp.float32),
        in_specs=[
            smem,
            smem,
            pl.BlockSpec((row_len, TOTAL), lambda i: (0, 0)),
            pl.BlockSpec(arrived.shape, lambda i: (0, 0, 0)),
        ],
        out_specs=pl.BlockSpec((row_len, TOTAL), lambda i: (0, 0)),
        compiler_params=pltpu.CompilerParams(vmem_limit_bytes=40 * MIB),
    )(codes, first, front, arrived)


def split(value):
    high = value.astype(jnp.bfloat16)
    low = (value - high.astype(jnp.float32)).astype(jnp.bfloat16)
    return high, low


def rows_kernel(raw_ref, inverse_ref, out_ref, high_ref, low_ref):
    solved = dot_nt(raw_ref[...], inverse_ref[...])
    out_ref[...] = solved
    high_ref[...], low_ref[...] = split(solved)


def solve_rows(raw, inverse):
    length = raw.shape[0]
    step = min(512, length)
    block = pl.BlockSpec((step, TOTAL), lambda i: (i, 0))
    return pl.pallas_call(
        rows_kernel,
        grid=(length // step,),
        out_shape=[
            jax.ShapeDtypeStruct((length, TOTAL), jnp.float32),
            jax.ShapeDtypeStruct((length, TOTAL), jnp.bfloat16),
            jax.ShapeDtypeStruct((length, TOTAL), jnp.bfloat16),
        ],
        in_specs=[block, pl.BlockSpec((TOTAL, TOTAL), lambda i: (0, 0))],
        out_specs=[block, block, block],
        compiler_params=pltpu.CompilerParams(vmem_limit_bytes=24 * MIB),
    )(raw, inverse)


def cols_kernel(raw_ref, inverse_ref, out_ref, high_ref, low_ref):
    solved = dot_nt(inverse_ref[...], raw_ref[...])
    out_ref[...] = solved
    high_ref[...], low_ref[...] = split(solved)


def solve_cols(raw, inverse):
    length = raw.shape[0]
    step = min(512, length)
    block = pl.BlockSpec((TOTAL, step), lambda i: (0, i))
    return pl.pallas_call(
        cols_kernel,
        grid=(length // step,),
        out_shape=[
            jax.ShapeDtypeStruct((TOTAL, length), jnp.float32),
            jax.ShapeDtypeStruct((TOTAL, length), jnp.bfloat16),
            jax.ShapeDtypeStruct((TOTAL, length), jnp.bfloat16),
        ],
        in_specs=[
            pl.BlockSpec((step, TOTAL), lambda i: (i, 0)),
            pl.BlockSpec((TOTAL, TOTAL), lambda i: (0, 0)),
        ],
        out_specs=[block, block, block],
        compiler_params=pltpu.CompilerParams(vmem_limit_bytes=24 * MIB),
    )(raw, inverse)


def final_kernel(
    cols_blocks, code_ref, place_ref, front_ref, rows_ref, rows_high, rows_low, cols_ref, cols_high,
    cols_low, lower_ref, arrived_ref, out_ref, cursor
):
    step = pl.program_id(0)
    sources, capacity = code_ref.shape
    height, width = front_ref.shape
    side = arrived_ref.shape[1]
    per_step = height // side

    @pl.when(step == 0)
    def _():
        for s in range(sources):
            cursor[s] = 0

    chunk = min(512, width)
    for start in range(0, width, chunk):
        at = slice(start, start + chunk)
        change = jnp.dot(rows_high[...], cols_high[:, at], preferred_element_type=jnp.float32)
        change += jnp.dot(rows_high[...], cols_low[:, at], preferred_element_type=jnp.float32)
        change += jnp.dot(rows_low[...], cols_high[:, at], preferred_element_type=jnp.float32)
        out_ref[:, at] = front_ref[:, at] - change

    edge = (step + 1) * per_step * cols_blocks

    @pl.loop(0, sources)
    def _(s):
        def more(k):
            code = code_ref[s, jnp.minimum(k, capacity - 1)]
            return (k < capacity) & (code >= 0) & (code < edge)

        def add(k):
            code = code_ref[s, k]
            block_row = code // cols_blocks - step * per_step
            block_col = code % cols_blocks
            rows = pl.ds(pl.multiple_of(block_row * side, side), side)
            columns = pl.ds(pl.multiple_of(block_col * side, side), side)
            out_ref[rows, columns] += arrived_ref[s * capacity + k]
            return k + 1

        cursor[s] = lax.while_loop(more, add, cursor[s])

    top = (place_ref[0] == 0) & (step == 0)

    @pl.when(top)
    def _():
        out_ref[...] = cols_ref[...]

    @pl.when(place_ref[1] == 0)
    def _():
        out_ref[:, :TOTAL] = jnp.where(top, lower_ref[...], rows_ref[...])


def finish(front, rows, cols, lower, arrived, codes, place, cols_blocks):
    row_len, col_len = front.shape
    height = TOTAL
    smem = pl.BlockSpec(memory_space=pltpu.SMEM)
    block = pl.BlockSpec((height, TOTAL), lambda i: (i, 0))
    wide = pl.BlockSpec((height, col_len), lambda i: (i, 0))
    whole = pl.BlockSpec((TOTAL, col_len), lambda i: (0, 0))
    return pl.pallas_call(
        functools.partial(final_kernel, cols_blocks),
        grid=(row_len // height,),
        out_shape=jax.ShapeDtypeStruct((row_len, col_len), jnp.float32),
        in_specs=[
            smem, smem, wide, block, block, block, whole, whole, whole,
            pl.BlockSpec((TOTAL, TOTAL), lambda i: (0, 0)),
            pl.BlockSpec(memory_space=pltpu.VMEM),
        ],
        out_specs=wide,
        scratch_shapes=[pltpu.SMEM((codes.shape[0],), jnp.int32)],
        compiler_params=pltpu.CompilerParams(vmem_limit_bytes=56 * MIB),
    )(codes, place, front, *rows, *cols, lower, arrived)


def factor(diagonal):
    def lower_of(block):
        return jnp.linalg.cholesky(jnp.tril(block) + jnp.tril(block, -1).T)

    def inverse_of(block):
        return jax.scipy.linalg.solve_triangular(block, jnp.eye(NB, dtype=jnp.float32), lower=True)

    first = lower_of(diagonal[:NB, :NB])
    first_inverse = inverse_of(first)
    below = dot_nt(diagonal[NB:, :NB], first_inverse)
    second = lower_of(diagonal[NB:, NB:] - dot_nt(below, below))
    second_inverse = inverse_of(second)
    corner = -jnp.dot(second_inverse, jnp.dot(below, first_inverse, precision=precise), precision=precise)
    zero = jnp.zeros((NB, NB), jnp.float32)
    return jnp.block([[first, zero], [below, second]]), jnp.block([[first_inverse, zero], [corner, second_inverse]])


def body(front, tiles, tile_block, valid_rows):
    row_len, col_len = front.shape
    row_count = lax.axis_size("row")
    col_count = lax.axis_size("col")
    device_count = row_count * col_count
    per_device = tiles.shape[0]
    side = tiles.shape[1]
    capacity = 2 * per_device // device_count
    rows_blocks = row_len // side
    cols_blocks = col_len // side
    row_now = lax.axis_index("row")
    col_now = lax.axis_index("col")
    device_now = row_now * col_count + col_now

    block_row = tile_block[0].reshape(device_count, per_device)
    block_col = tile_block[1].reshape(device_count, per_device)
    target_row = block_row // rows_blocks
    target = target_row * col_count + block_col // cols_blocks
    code = block_row % rows_blocks * cols_blocks + block_col % cols_blocks
    position = lax.broadcasted_iota(jnp.int32, target.shape, 1)
    place = jnp.stack([row_now, col_now]).astype(jnp.int32)

    def own(values):
        return lax.dynamic_index_in_dim(values, device_now, 0, keepdims=False)

    in_panel = block_col < PANELS
    panel_key = jnp.where(in_panel, target_row, -1)
    panel_rank = jnp.sum(
        (panel_key[:, :, None] == panel_key[:, None, :]) & (position[:, None, :] < position[:, :, None]),
        axis=2,
    )
    ahead = (own(target_row) - row_now) % row_count
    panel_slot = jnp.where(own(in_panel), ahead * capacity + own(panel_rank), -1)
    panel_out = pack(tiles, panel_slot, valid_rows, row_count * capacity)
    panel_in = [panel_out[:capacity]]
    for shift in range(1, row_count):
        sending = panel_out[shift * capacity : (shift + 1) * capacity]
        turn = [(r, (r + shift) % row_count) for r in range(row_count)]
        panel_in.append(lax.ppermute(sending, "row", turn))
    same_col = lax.dynamic_index_in_dim(
        jnp.stack([panel_key, panel_rank, code]).reshape(3, row_count, col_count, per_device),
        col_now, 2, keepdims=False,
    )
    slots = jnp.arange(capacity)
    fits = (same_col[0] == row_now)[:, :, None] & (same_col[1][:, :, None] == slots)
    panel_code = same_col[2] // cols_blocks * PANELS + same_col[2] % cols_blocks
    panel_codes = jnp.sum(jnp.where(fits, panel_code[:, :, None] + 1, 0), axis=1) - 1
    by_shift = (row_now - jnp.arange(row_count)) % row_count
    panel_codes = jnp.take(panel_codes, by_shift, axis=0).reshape(-1)

    order = (target * rows_blocks * cols_blocks + code) * per_device + position
    ranking = jnp.sum(
        (target[:, :, None] == target[:, None, :]) & (order[:, None, :] < order[:, :, None]), axis=2
    )
    slot = own(target) * capacity + own(ranking)
    here = (target == device_now)[:, :, None] & (ranking[:, :, None] == slots)
    codes = jnp.sum(jnp.where(here, code[:, :, None] + 1, 0), axis=1) - 1
    outgoing = pack(tiles, slot, valid_rows, device_count * capacity)
    arrived = lax.all_to_all(
        outgoing.reshape(device_count, capacity, side, side), ("row", "col"), 0, 0, tiled=True
    ).reshape(device_count * capacity, side, side)

    first = (col_now == 0).astype(jnp.int32).reshape(1)
    partial = raw_panel(front, jnp.concatenate(panel_in, 0), panel_codes, first)
    raw_rows = lax.psum(partial, "col")
    slice_start = col_now * col_len % row_len
    slice_root = col_now * col_len // row_len
    picked = lax.dynamic_slice_in_dim(raw_rows, slice_start, col_len, 0)
    raw_cols = lax.psum(jnp.where(row_now == slice_root, picked, 0.0), "row")
    diagonal = jnp.where(row_now == 0, raw_rows[:TOTAL], jnp.eye(TOTAL, dtype=jnp.float32))
    lower, inverse = factor(diagonal)
    inverse = lax.psum(jnp.where(row_now == 0, inverse, 0.0), "row")
    rows = solve_rows(raw_rows, inverse)
    cols = solve_cols(raw_cols, inverse)
    return finish(front, rows, cols, lower, arrived, codes, place, cols_blocks)


def solution(mesh):
    placed = (P("row", "col"), P(("row", "col"), None, None), P(), P(("row", "col")))
    return jax.shard_map(
        body, mesh=mesh, in_specs=placed, out_specs=P("row", "col"), check_vma=False
    )
```

time: 997 us -> 781 us (0.78)
  local copies, waits for them, and re-layouts: 224 us -> 30.7 us
  Pallas kernels: 0 us -> 93.6 us
  other arithmetic: 122 us -> 58.4 us
  matrix products: 59 us -> 1.67 us
    ppermute x0 -> x3, waiting for transfers between devices: none -> 392 us  [body(): panel_in.append(lax.ppermute(sending, 'row', turn))]
    all_to_all x1, waiting for transfers between devices: 301 us -> 0.01 us  [body(): lax.all_to_all(outgoing.reshape(device_count, capacity, side, side), ('ro...]
    pallas_call x0 -> x6, Pallas kernels: none -> 93.6 us  [the longest x1 44.9 us: finish(): pl.pallas_call(functools.partial(final_kernel, cols_blocks), grid=(row_le...]
    psum x5 -> x2, waiting for transfers between devices: 261 us -> 177 us  [the longest x1 94.2 us: body(): inverse = lax.psum(jnp.where(row_now == 0, inverse, 0.0), 'row')]
    scatter x4 -> x0, local copies, waits for them, and re-layouts: 56.1 us -> none  [the longest x1 23.4 us: body(): outgoing = outgoing.at[own_target * capacity + own_rank].set(masked)]
    scatter-add x1 -> x0, other arithmetic: 54.5 us -> none  [body(): blocked = blocked.at[slot_row, :, slot_col, :].add(arrived)]
    dot_general x2 -> x4, matrix products: 50 us -> 1.13 us  [the longest x2 0.55 us: dot_nt(): lax.dot_general(a, b, (((1,), (1,)), ((), ())), precision=precision, pref...]
    unnamed x10 -> x32, local copies, waits for them, and re-layouts: 66.7 us -> 28.2 us
  transfers between devices with their start and end apart: 6 -> 6, of which waited for: 6 -> 4; matrix products, arithmetic and copies ran while one was open for 7% -> 8% of each run, Pallas kernels for 0% -> 2%
where the time goes in v1:
time: 781 us; the launch traced here: 778 us
  waiting for transfers between devices  569 us (73%)
  Pallas kernels  93.6 us (12%)
  other arithmetic  58.4 us (7%)
  local copies, waits for them, and re-layouts  30.7 us (4%)
  between operations  13.9 us (2%)
  starting transfers between devices  10.7 us (1%)
    ppermute x3, waiting for transfers between devices, body(): panel_in.append(lax.ppermute(sending, 'row', turn))  392 us
    psum x1, waiting for transfers between devices, body(): inverse = lax.psum(jnp.where(row_now == 0, inverse, 0.0), 'row')  94.2 us
    psum x1, waiting for transfers between devices, body(): raw_rows = lax.psum(partial, 'col')  82.8 us
    pallas_call x1, Pallas kernels, finish(): pl.pallas_call(functools.partial(final_kernel, cols_blocks), grid=(row_le...  44.9 us
    pallas_call x2, Pallas kernels, pack(): pl.pallas_call(pack_kernel, out_shape=jax.ShapeDtypeStruct((n_slots, side...  37.6 us
    unnamed x32, local copies, waits for them, and re-layouts  28.2 us
    another operation x6, other arithmetic, lower_of(): return jnp.linalg.cholesky(jnp.tril(block) + jnp.tril(block, -1).T)  24.9 us
    another operation x5, other arithmetic, inverse_of(): jax.scipy.linalg.solve_triangular(block, jnp.eye(NB, dtype=jnp.float32),...  21.1 us
  transfers between devices with their start and end apart: 6, of which 4 were waited for; matrix products, arithmetic and copies ran while one was open for 8% of the time, Pallas kernels for 2%

profile of v1, /device:TPU:7, one launch (start us, length us, event | category | flops | bytes accessed | tf_op | source)
XLA Modules:
  0.0 778.4 jit_solution(4940895050380253772)
XLA Ops:
  7.5 2.0 convert_reduce_fusion.1
  9.6 3.4 copy-done.1
  13.6 29.9 %shard_map.50 = f32[256,128,128]{2,1,0:T(8,128)S(1)} custom-call(s32[128]{0:T(128)S(1)} %fusion.49.slot_ref, s32[128]{0:T(128)S(1)} %copy-done.14, f32[128,128,128]{2,1,0:T(8,128)S(1)} %copy-done.1), custom_call_target="tpu_custom_call" | custom-call | tf_op jit(solution)/shard_map/pallas_call | solution.py:55
  43.5 6.2 copy-done
  49.7 6.4 all-to-all-start
  56.2 1.3 convert_reduce_fusion
  57.5 3.4 copy-done.2
  60.9 7.7 shard_map.46
  68.7 3.7 collective-permute-start.2
  73.8 267.3 %collective-permute-done.2 = f32[8,128,128]{2,1,0:T(8,128)S(1)} collective-permute-done((f32[8,128,128]{2,1,0:T(8,128)S(1)}, f32[8,128,128]{2,1,0:T(8,128)S(1)}, u32[]{:S(2)}, u32[]{:S(2)}) %collective-permute-start.2) | collective-permute-done | bytes 524320 | tf_op jit(solution)/shard_map/ppermute | solution.py:296
  341.1 125.0 %collective-permute-done.1 = f32[8,128,128]{2,1,0:T(8,128)S(1)} collective-permute-done((f32[8,128,128]{2,1,0:T(8,128)S(1)}, f32[8,128,128]{2,1,0:T(8,128)S(1)}, u32[]{:S(2)}, u32[]{:S(2)}) %collective-permute-start.1) | collective-permute-done | bytes 524320 | tf_op jit(solution)/shard_map/ppermute | solution.py:296
  466.1 1.2 pad_maximum_fusion.arrived_ref
  467.3 3.3 shard_map.47
  470.6 2.0 copy-done.3
  473.1 82.8 %all-reduce.6.cloned.1.call-done.raw_ref = f32[4096,256]{1,0:T(8,128)} async-done(((f32[4096,256]{1,0:T(8,128)}), f32[4096,256]{1,0:T(8,128)}) %all-reduce.6.cloned.1.call-update) | async-done | bytes 4194320 | tf_op jit(solution)/shard_map/psum | solution.py:322
  557.2 11.7 %cholesky.44 = f32[128,128]{1,0:T(8,128)S(1)} custom-call(f32[128,128]{1,0:T(8,128)S(1)} %copy.50), custom_call_target="Cholesky" | custom-call | tf_op jit(solution)/shard_map/jit(cholesky)/cholesky | solution.py:243
  570.4 9.8 %custom-call.6 = f32[1,128,128]{1,2,0:T(8,128)S(1)} custom-call(f32[1,128,128]{2,1,0:T(8,128)S(1)} %get-tuple-element.23), custom_call_target="InvertDiagBlocksLowerTriangular" | custom-call | tf_op jit(solution)/shard_map/jit(_solve_triangular)/triangular_solve | solution.py:246
  581.3 11.7 %cholesky.55 = f32[128,128]{1,0:T(8,128)S(1)} custom-call(f32[128,128]{1,0:T(8,128)S(1)} %fusion.10), custom_call_target="Cholesky" | custom-call | tf_op jit(solution)/shard_map/jit(cholesky)/cholesky | solution.py:243
  594.4 10.0 %custom-call.7 = f32[1,128,128]{1,2,0:T(8,128)S(1)} custom-call(f32[1,128,128]{2,1,0:T(8,128)S(1)} %get-tuple-element.21), custom_call_target="InvertDiagBlocksLowerTriangular" | custom-call | tf_op jit(solution)/shard_map/jit(_solve_triangular)/triangular_solve | solution.py:246
  606.1 3.1 dynamic-slice_select_fusion
  611.8 94.2 %all-reduce.8.cloned.1.call-done = (f32[256,256]{1,0:T(8,128)}, f32[2048,256]{1,0:T(8,128)}) async-done(((f32[256,256]{1,0:T(8,128)}, f32[2048,256]{1,0:T(8,128)}), (f32[256,256]{1,0:T(8,128)}, f32[2048,256]{1,0:T(8,128)})) %all-reduce.8.cloned.1.call-update) | async-done | bytes 2359312 | tf_op jit(solution)/shard_map/psum | solution.py:329
  706.1 1.6 copy-done.9
  708.6 2.8 shard_map.49
  711.5 1.3 copy-done.6
  712.8 1.0 copy-done.10
  713.8 1.0 copy-done.11
  714.8 2.2 copy-done.4
  717.0 5.1 shard_map.48
  722.0 1.9 copy-done.5
  724.0 1.4 copy-done.7
  725.3 1.4 copy-done.8
  726.7 44.9 %shard_map.51 = f32[4096,2048]{1,0:T(8,128)} custom-call(s32[32,8]{1,0:T(8,128)} %broadcast_add_fusion.code_ref, s32[2]{0:T(128)} %pad_add_fusion.place_ref, f32[4096,2048]{1,0:T(8,128)} %front_ref.3, f32[4096,256]{1,0:T(8,128)} %copy-done.5, bf16[4096,256]{1,0:T(8,128)(2,1)} %copy-done.7, bf16[4096,256]{1,0:T(8,128)(2,1)} %copy-done.8, ...), custom_call_target="tpu_custom_call" | custom-call | tf_op jit(solution)/shard_map/pallas_call | solution.py:226
  (84 shorter events, 14.1 us)
Async XLA Ops:
  9.5 3.4 copy-start.1
  12.9 0.7 copy-start.14
  43.5 6.2 copy-start
  49.7 7.8 %copy-start.15 = (s32[128]{0:T(128)S(1)}, s32[128]{0:T(128)}, u32[]{:S(2)}) copy-start(s32[128]{0:T(128)} %valid_ref.3) | copy-start | bytes 1540
  49.7 677.0 %all-to-all-start = ((f32[32,8,128,128]{3,2,1,0:T(8,128)}), f32[32,8,128,128]{3,2,1,0:T(8,128)}, u32[]{:S(2)}, u32[]{:S(2)}) async-start(f32[32,8,128,128]{3,2,1,0:T(8,128)} %bitcast.63), calls=%async_computation | async-start | bytes 33554432 | tf_op jit(solution)/shard_map/all_to_all | solution.py:316
  56.1 499.8 %all-reduce.6.cloned.1.call-start = ((), (), s32[]{:S(2)}) async-start(), calls=%async_computation.1 | async-start | bytes 8388608 | tf_op jit(solution)/shard_map/psum | solution.py:322
  57.5 3.4 copy-start.2
  68.7 272.4 %collective-permute-start.2 = (f32[8,128,128]{2,1,0:T(8,128)S(1)}, f32[8,128,128]{2,1,0:T(8,128)S(1)}, u32[]{:S(2)}, u32[]{:S(2)}) collective-permute-start(f32[8,128,128]{2,1,0:T(8,128)S(1)} %get-tuple-element.32), channel_id=1, source_target_pairs={{0,24},{8,0},{16,8},{24,16},{1,25},{9,1},{17,9},{25,17},{2,26},{10... | collective-permute-start | bytes 1572872 | tf_op jit(solution)/shard_map/ppermute | solution.py:296
  72.4 393.7 %collective-permute-start.1 = (f32[8,128,128]{2,1,0:T(8,128)S(1)}, f32[8,128,128]{2,1,0:T(8,128)S(1)}, u32[]{:S(2)}, u32[]{:S(2)}) collective-permute-start(f32[8,128,128]{2,1,0:T(8,128)S(1)} %get-tuple-element.33), channel_id=1, source_target_pairs={{0,16},{8,24},{16,0},{24,8},{1,17},{9,25},{17,1},{25,9},{2,18},{10... | collective-permute-start | bytes 1572872 | tf_op jit(solution)/shard_map/ppermute | solution.py:296
  72.4 393.7 %collective-permute-start = (f32[8,128,128]{2,1,0:T(8,128)S(1)}, f32[8,128,128]{2,1,0:T(8,128)}, u32[]{:S(2)}, u32[]{:S(2)}) collective-permute-start(f32[8,128,128]{2,1,0:T(8,128)S(1)} %get-tuple-element.34), channel_id=1, source_target_pairs={{0,8},{8,16},{16,24},{24,0},{1,9},{9,17},{17,25},{25,1},{2,10},{10... | collective-permute-start | bytes 1572872 | tf_op jit(solution)/shard_map/ppermute | solution.py:296
  470.5 2.0 copy-start.3
  472.6 233.5 %all-reduce.8.cloned.1.call-start = ((), (), s32[]{:S(2)}) async-start(), calls=%async_computation.2 | async-start | bytes 4718592 | tf_op jit(solution)/shard_map/psum | solution.py:329
  706.1 1.6 copy-start.9
  707.7 0.9 copy-start.12
  708.6 6.2 copy-start.13
  711.5 1.3 copy-start.6
  712.8 1.0 copy-start.10
  713.8 1.0 copy-start.11
  714.8 2.2 copy-start.4
  722.0 1.9 copy-start.5
  724.0 1.4 copy-start.7
  725.3 1.4 copy-start.8
Sparse Core Ops, SparseCore 0:
  472.7 83.1 all-reduce.5
  609.3 96.7 all-reduce.7

commit v2 on v1

--- a/solution.py
+++ b/solution.py
@@ -22,14 +22,12 @@
     )
 
 
-def pack_kernel(slot_ref, valid_ref, tiles_ref, out_ref, buf, sem_in, sem_out):
+def pack_kernel(slot_ref, valid_ref, tiles_ref, out_ref, buf, sem):
     count, side = tiles_ref.shape[0], tiles_ref.shape[1]
-
-    def fetch(t):
-        return pltpu.make_async_copy(tiles_ref.at[t], buf.at[t], sem_in.at[t])
+    half = side // 2
 
     def store(t):
-        return pltpu.make_async_copy(buf.at[t], out_ref.at[jnp.maximum(slot_ref[t], 0)], sem_out.at[t])
+        return pltpu.make_async_copy(buf.at[t], out_ref.at[jnp.maximum(slot_ref[t], 0)], sem.at[t])
 
     def each(act):
         @pl.loop(0, count)
@@ -39,12 +37,11 @@
                 act(t)
 
     def mask(t):
-        fetch(t).wait()
-        rows = lax.broadcasted_iota(jnp.int32, (side, side), 0)
-        buf[t] = jnp.where(rows < valid_ref[t], buf[t], 0.0)
+        rows = lax.broadcasted_iota(jnp.int32, (half, side), 0) + half
+        buf[t, :half] = tiles_ref[t, :half]
+        buf[t, half:] = jnp.where(rows < valid_ref[t], tiles_ref[t, half:], 0.0)
         store(t).start()
 
-    each(lambda t: fetch(t).start())
     each(mask)
     each(lambda t: store(t).wait())
 
@@ -55,11 +52,10 @@
     return pl.pallas_call(
         pack_kernel,
         out_shape=jax.ShapeDtypeStruct((n_slots, side, side), jnp.float32),
-        in_specs=[smem, smem, pl.BlockSpec(memory_space=pl.ANY)],
+        in_specs=[smem, smem, pl.BlockSpec(memory_space=pltpu.VMEM)],
         out_specs=pl.BlockSpec(memory_space=pl.ANY),
         scratch_shapes=[
             pltpu.VMEM((count, side, side), jnp.float32),
-            pltpu.SemaphoreType.DMA((count,)),
             pltpu.SemaphoreType.DMA((count,)),
         ],
         compiler_params=pltpu.CompilerParams(vmem_limit_bytes=24 * MIB),
@@ -313,6 +309,7 @@
     here = (target == device_now)[:, :, None] & (ranking[:, :, None] == slots)
     codes = jnp.sum(jnp.where(here, code[:, :, None] + 1, 0), axis=1) - 1
     outgoing = pack(tiles, slot, valid_rows, device_count * capacity)
+    outgoing, *panel_in = lax.optimization_barrier((outgoing, *panel_in))
     arrived = lax.all_to_all(
         outgoing.reshape(device_count, capacity, side, side), ("row", "col"), 0, 0, tiled=True
     ).reshape(device_count * capacity, side, side)

time: 781 us -> 601 us (0.77)
  the two profiles are of different devices: /device:TPU:7 before, /device:TPU:0 now
where the time goes in v2:
time: 601 us; the launch traced here: 599 us
  waiting for transfers between devices  411 us (68%)
  Pallas kernels  77.1 us (13%)
  other arithmetic  57.3 us (10%)
  local copies, waits for them, and re-layouts  27.4 us (5%)
  between operations  13.9 us (2%)
  starting transfers between devices  11.2 us (2%)
    psum x1, waiting for transfers between devices, body(): raw_rows = lax.psum(partial, 'col')  238 us
    psum x1, waiting for transfers between devices, body(): inverse = lax.psum(jnp.where(row_now == 0, inverse, 0.0), 'row')  153 us
    pallas_call x1, Pallas kernels, finish(): pl.pallas_call(functools.partial(final_kernel, cols_blocks), grid=(row_le...  44.8 us
    another operation x6, other arithmetic, lower_of(): return jnp.linalg.cholesky(jnp.tril(block) + jnp.tril(block, -1).T)  24.9 us
    unnamed x32, local copies, waits for them, and re-layouts  24.8 us
    another operation x5, other arithmetic, inverse_of(): jax.scipy.linalg.solve_triangular(block, jnp.eye(NB, dtype=jnp.float32),...  21.1 us
    pallas_call x2, Pallas kernels, pack(): pl.pallas_call(pack_kernel, out_shape=jax.ShapeDtypeStruct((n_slots, side...  21.1 us
    ppermute x3, waiting for transfers between devices, body(): panel_in.append(lax.ppermute(sending, 'row', turn))  19.5 us
  transfers between devices with their start and end apart: 6, of which 3 were waited for; matrix products, arithmetic and copies ran while one was open for 10% of the time, Pallas kernels for 5%

profile of v2, /device:TPU:0, one launch (start us, length us, event | category | flops | bytes accessed | tf_op | source)
XLA Modules:
  0.0 599.2 jit_solution(13275811927444314146)
XLA Ops:
  6.5 0.9 fusion.54
  7.5 1.3 convert_reduce_fusion
  8.8 3.4 copy-done.1
  12.8 5.0 shard_map.47
  18.0 5.4 collective-permute-start.2
  24.0 2.0 convert_reduce_fusion.1
  26.1 16.1 %shard_map.46 = f32[256,128,128]{2,1,0:T(8,128)S(1)} custom-call(s32[128]{0:T(128)S(1)} %fusion.49.slot_ref, s32[128]{0:T(128)S(1)} %copy-done.15, f32[128,128,128]{2,1,0:T(8,128)S(1)} %copy-done.2), custom_call_target="tpu_custom_call" | custom-call | tf_op jit(solution)/shard_map/pallas_call | solution.py:52
  42.2 6.2 %copy-done = f32[256,128,128]{2,1,0:T(8,128)} copy-done((f32[256,128,128]{2,1,0:T(8,128)}, f32[256,128,128]{2,1,0:T(8,128)S(1)}, u32[]{:S(2)}) %copy-start) | copy-done | bytes 16777240
  48.4 19.5 %collective-permute-done.1 = f32[8,128,128]{2,1,0:T(8,128)S(1)} collective-permute-done((f32[8,128,128]{2,1,0:T(8,128)S(1)}, f32[8,128,128]{2,1,0:T(8,128)S(1)}, u32[]{:S(2)}, u32[]{:S(2)}) %collective-permute-start.1) | collective-permute-done | bytes 524320 | tf_op jit(solution)/shard_map/ppermute | solution.py:292
  67.9 4.9 all-to-all-start
  74.1 3.3 shard_map.48
  77.3 2.0 copy-done.3
  79.9 238.0 %all-reduce.6.cloned.1.call-done.raw_ref = f32[4096,256]{1,0:T(8,128)} async-done(((f32[4096,256]{1,0:T(8,128)}), f32[4096,256]{1,0:T(8,128)}) %all-reduce.6.cloned.1.call-update) | async-done | bytes 4194320 | tf_op jit(solution)/shard_map/psum | solution.py:319
  317.9 1.0 slice_select_fusion
  319.2 11.7 %cholesky.44 = f32[128,128]{1,0:T(8,128)S(1)} custom-call(f32[128,128]{1,0:T(8,128)S(1)} %copy.50), custom_call_target="Cholesky" | custom-call | tf_op jit(solution)/shard_map/jit(cholesky)/cholesky | solution.py:239
  332.4 9.8 %custom-call.6 = f32[1,128,128]{1,2,0:T(8,128)S(1)} custom-call(f32[1,128,128]{2,1,0:T(8,128)S(1)} %get-tuple-element.33), custom_call_target="InvertDiagBlocksLowerTriangular" | custom-call | tf_op jit(solution)/shard_map/jit(_solve_triangular)/triangular_solve | solution.py:242
  343.3 11.7 %cholesky.55 = f32[128,128]{1,0:T(8,128)S(1)} custom-call(f32[128,128]{1,0:T(8,128)S(1)} %fusion.10), custom_call_target="Cholesky" | custom-call | tf_op jit(solution)/shard_map/jit(cholesky)/cholesky | solution.py:239
  356.4 10.0 %custom-call.7 = f32[1,128,128]{1,2,0:T(8,128)S(1)} custom-call(f32[1,128,128]{2,1,0:T(8,128)S(1)} %get-tuple-element.31), custom_call_target="InvertDiagBlocksLowerTriangular" | custom-call | tf_op jit(solution)/shard_map/jit(_solve_triangular)/triangular_solve | solution.py:242
  368.1 3.1 dynamic-slice_select_fusion
  373.8 153.1 %all-reduce.8.cloned.1.call-done = (f32[256,256]{1,0:T(8,128)}, f32[2048,256]{1,0:T(8,128)}) async-done(((f32[256,256]{1,0:T(8,128)}, f32[2048,256]{1,0:T(8,128)}), (f32[256,256]{1,0:T(8,128)}, f32[2048,256]{1,0:T(8,128)})) %all-reduce.8.cloned.1.call-update) | async-done | bytes 2359312 | tf_op jit(solution)/shard_map/psum | solution.py:326
  527.0 1.6 copy-done.9
  528.6 0.9 copy-done.12
  529.5 2.8 shard_map.50
  532.4 1.3 copy-done.6
  533.7 1.0 copy-done.10
  534.7 1.0 copy-done.11
  535.7 2.2 copy-done.4
  537.9 5.1 shard_map.49
  542.9 1.9 copy-done.5
  544.9 1.4 copy-done.7
  546.2 1.4 copy-done.8
  547.6 44.8 %shard_map.51 = f32[4096,2048]{1,0:T(8,128)} custom-call(s32[32,8]{1,0:T(8,128)} %broadcast_add_fusion.code_ref, s32[2]{0:T(128)} %pad_add_fusion.place_ref, f32[4096,2048]{1,0:T(8,128)} %front_ref.3, f32[4096,256]{1,0:T(8,128)} %copy-done.5, bf16[4096,256]{1,0:T(8,128)(2,1)} %copy-done.7, bf16[4096,256]{1,0:T(8,128)(2,1)} %copy-done.8, ...), custom_call_target="tpu_custom_call" | custom-call | tf_op jit(solution)/shard_map/pallas_call | solution.py:222
  (84 shorter events, 11.7 us)
Async XLA Ops:
  8.8 3.4 copy-start.1
  12.2 0.7 copy-start.14
  12.8 13.2 %copy-start.2 = (f32[128,128,128]{2,1,0:T(8,128)S(1)}, f32[128,128,128]{2,1,0:T(8,128)}, u32[]{:S(2)}) copy-start(f32[128,128,128]{2,1,0:T(8,128)} %tiles_ref.3) | copy-start | bytes 25165828
  17.8 8.3 %copy-start.15 = (s32[128]{0:T(128)S(1)}, s32[128]{0:T(128)}, u32[]{:S(2)}) copy-start(s32[128]{0:T(128)} %valid_ref.3) | copy-start | bytes 1540
  18.0 30.4 %collective-permute-start.2 = (f32[8,128,128]{2,1,0:T(8,128)S(1)}, f32[8,128,128]{2,1,0:T(8,128)S(1)}, u32[]{:S(2)}, u32[]{:S(2)}) collective-permute-start(f32[8,128,128]{2,1,0:T(8,128)S(1)} %get-tuple-element.41), channel_id=1, source_target_pairs={{0,24},{8,0},{16,8},{24,16},{1,25},{9,1},{17,9},{25,17},{2,26},{10... | collective-permute-start | bytes 1572872 | tf_op jit(solution)/shard_map/ppermute | solution.py:292
  23.4 44.5 %collective-permute-start.1 = (f32[8,128,128]{2,1,0:T(8,128)S(1)}, f32[8,128,128]{2,1,0:T(8,128)S(1)}, u32[]{:S(2)}, u32[]{:S(2)}) collective-permute-start(f32[8,128,128]{2,1,0:T(8,128)S(1)} %get-tuple-element.42), channel_id=1, source_target_pairs={{0,16},{8,24},{16,0},{24,8},{1,17},{9,25},{17,1},{25,9},{2,18},{10... | collective-permute-start | bytes 1572872 | tf_op jit(solution)/shard_map/ppermute | solution.py:292
  23.4 44.5 %collective-permute-start = (f32[8,128,128]{2,1,0:T(8,128)S(1)}, f32[8,128,128]{2,1,0:T(8,128)S(1)}, u32[]{:S(2)}, u32[]{:S(2)}) collective-permute-start(f32[8,128,128]{2,1,0:T(8,128)S(1)} %get-tuple-element.43), channel_id=1, source_target_pairs={{0,8},{8,16},{16,24},{24,0},{1,9},{9,17},{17,25},{25,1},{2,10},{10... | collective-permute-start | bytes 1572872 | tf_op jit(solution)/shard_map/ppermute | solution.py:292
  42.2 6.2 %copy-start = (f32[256,128,128]{2,1,0:T(8,128)}, f32[256,128,128]{2,1,0:T(8,128)S(1)}, u32[]{:S(2)}) copy-start(f32[256,128,128]{2,1,0:T(8,128)S(1)} %shard_map.46) | copy-start | bytes 50331652
  67.9 479.7 %all-to-all-start = ((f32[32,8,128,128]{3,2,1,0:T(8,128)}), f32[32,8,128,128]{3,2,1,0:T(8,128)}, u32[]{:S(2)}, u32[]{:S(2)}) async-start(f32[32,8,128,128]{3,2,1,0:T(8,128)} %bitcast.63), calls=%async_computation | async-start | bytes 33554432 | tf_op jit(solution)/shard_map/all_to_all | solution.py:313
  72.8 245.1 %all-reduce.6.cloned.1.call-start = ((), (), s32[]{:S(2)}) async-start(), calls=%async_computation.1 | async-start | bytes 8388608 | tf_op jit(solution)/shard_map/psum | solution.py:319
  77.3 2.0 copy-start.3
  79.3 447.6 %all-reduce.8.cloned.1.call-start = ((), (), s32[]{:S(2)}) async-start(), calls=%async_computation.2 | async-start | bytes 4718592 | tf_op jit(solution)/shard_map/psum | solution.py:326
  527.0 1.6 copy-start.9
  528.6 0.9 copy-start.12
  529.5 6.2 %copy-start.13 = (f32[256,256]{1,0:T(8,128)S(1)}, f32[256,256]{1,0:T(8,128)}, u32[]{:S(2)}) copy-start(f32[256,256]{1,0:T(8,128)} %get-tuple-element.29.inverse_ref) | copy-start | bytes 786436
  532.4 1.3 copy-start.6
  533.7 1.0 copy-start.10
  534.7 1.0 copy-start.11
  535.7 2.2 copy-start.4
  542.9 1.9 copy-start.5
  544.9 1.4 copy-start.7
  546.2 1.4 copy-start.8
Sparse Core Ops, SparseCore 0:
  79.4 238.4 all-reduce.5
  371.3 155.6 all-reduce.7

commit v3 on v2

--- a/solution.py
+++ b/solution.py
@@ -11,6 +11,7 @@
 PANELS = 2
 TOTAL = NB * PANELS
 MIB = 1 << 20
+UNIT = 8
 
 
 precise = lax.Precision.HIGHEST
@@ -60,6 +61,154 @@
         ],
         compiler_params=pltpu.CompilerParams(vmem_limit_bytes=24 * MIB),
     )(slots, valid, tiles)
+
+
+def spread_kernel(
+    width, stride, meta_ref, empty_ref, count_ref, tiles_ref, out_ref, code_ref, stage, sem
+):
+    count, units = tiles_ref.shape[0], tiles_ref.shape[1]
+    devices, length = code_ref.shape
+
+    @pl.loop(0, devices)
+    def _(d):
+        for k in range(length):
+            code_ref[d, k] = -1
+
+    @pl.loop(0, count)
+    def _(i):
+        tile, target, base = meta_ref[0, i], meta_ref[1, i], meta_ref[2, i]
+        filled, code, valid = meta_ref[3, i], meta_ref[4, i], meta_ref[5, i]
+        shape = tiles_ref.shape[1:]
+        rows = lax.broadcasted_iota(jnp.int32, shape, 0) * shape[1]
+        rows += lax.broadcasted_iota(jnp.int32, shape, 1)
+        stage[target, pl.ds(base, units)] = jnp.where(rows < valid, tiles_ref[tile], 0.0)
+        for u in range(units):
+            code_ref[target, base + u] = jnp.where(u < filled, code + u * stride, -1)
+
+    for half in range(2):
+        first = 0 if half == 0 else count_ref[0]
+        last = count_ref[0] if half == 0 else count
+        free = count_ref[1 + half]
+
+        def each_tile(i, carry):
+            target, base, filled = meta_ref[1, i], meta_ref[2, i], meta_ref[3, i]
+
+            def each_unit(q, carry):
+                at, depth = carry
+                relay = empty_ref[half, at]
+                place = jnp.minimum(depth, width - 1)
+                stage[relay, place] = stage[target, q]
+                code_ref[relay, place] = code_ref[target, q]
+                wrap = at + 1 >= free
+                return jnp.where(wrap, 0, at + 1), jnp.where(wrap, depth + 1, depth)
+
+            return lax.fori_loop(jnp.maximum(base, width), base + filled, each_unit, carry)
+
+        lax.fori_loop(first, last, each_tile, (jnp.int32(0), jnp.int32(0)))
+
+    copy = pltpu.make_async_copy(stage.at[:, pl.ds(0, width)], out_ref, sem)
+    copy.start()
+    copy.wait()
+
+
+def spread(tiles, meta, empties, counts, devices, width, length, stride):
+    count, side = tiles.shape[0], tiles.shape[1]
+    units = side // UNIT
+    smem = pl.BlockSpec(memory_space=pltpu.SMEM)
+    return pl.pallas_call(
+        functools.partial(spread_kernel, width, stride),
+        out_shape=[
+            jax.ShapeDtypeStruct((devices, width, UNIT, side), jnp.float32),
+            jax.ShapeDtypeStruct((devices, length), jnp.int32),
+        ],
+        in_specs=[smem, smem, smem, pl.BlockSpec(memory_space=pltpu.VMEM)],
+        out_specs=[pl.BlockSpec(memory_space=pl.ANY), smem],
+        scratch_shapes=[
+            pltpu.VMEM((devices, length, UNIT, side), jnp.float32),
+            pltpu.SemaphoreType.DMA,
+        ],
+        compiler_params=pltpu.CompilerParams(vmem_limit_bytes=40 * MIB),
+    )(meta, empties, counts, tiles.reshape(count, units, UNIT, side))
+
+
+def relay_kernel(slot_ref, arrived_ref, out_ref):
+    devices, width = slot_ref.shape
+
+    @pl.loop(0, devices)
+    def _(s):
+        def more(k):
+            return (k < width) & (slot_ref[s, jnp.minimum(k, width - 1)] >= 0)
+
+        def move(k):
+            out_ref[slot_ref[s, k]] = arrived_ref[s, k]
+            return k + 1
+
+        lax.while_loop(more, move, jnp.int32(0))
+
+
+def relay(slots, arrived, length):
+    vmem = pl.BlockSpec(memory_space=pltpu.VMEM)
+    return pl.pallas_call(
+        relay_kernel,
+        out_shape=jax.ShapeDtypeStruct((length,) + arrived.shape[2:], jnp.float32),
+        in_specs=[pl.BlockSpec(memory_space=pltpu.SMEM), vmem],
+        out_specs=vmem,
+        compiler_params=pltpu.CompilerParams(vmem_limit_bytes=40 * MIB),
+    )(slots, arrived)
+
+
+def add_kernel(cols_blocks, code_ref, place_ref, partial_ref, arrived_ref, out_ref, cursor):
+    step = pl.program_id(0)
+    sources, capacity = code_ref.shape
+    unit, side = arrived_ref.shape[2:]
+    per_step = partial_ref.shape[0] // unit
+
+    @pl.when(step == 0)
+    def _():
+        for s in range(sources):
+            cursor[s] = 0
+
+    out_ref[...] = partial_ref[...]
+    edge = (step + 1) * per_step * cols_blocks
+
+    @pl.loop(0, sources)
+    def _(s):
+        def more(k):
+            code = code_ref[s, jnp.minimum(k, capacity - 1)]
+            return (k < capacity) & (code >= 0) & (code < edge)
+
+        def add(k):
+            code = code_ref[s, k]
+            unit_row = code // cols_blocks - step * per_step
+            block_col = code % cols_blocks
+            fixed = (place_ref[0] == 0) & (step == 0)
+            fixed |= (place_ref[1] == 0) & (block_col < PANELS)
+
+            @pl.when(jnp.logical_not(fixed))
+            def _():
+                rows = pl.ds(pl.multiple_of(unit_row * unit, unit), unit)
+                columns = pl.ds(pl.multiple_of(block_col * side, side), side)
+                out_ref[rows, columns] += arrived_ref[s, k]
+
+            return k + 1
+
+        cursor[s] = lax.while_loop(more, add, cursor[s])
+
+
+def add_relayed(partial, arrived, codes, place, cols_blocks):
+    row_len, col_len = partial.shape
+    smem = pl.BlockSpec(memory_space=pltpu.SMEM)
+    wide = pl.BlockSpec((TOTAL, col_len), lambda i: (i, 0))
+    return pl.pallas_call(
+        functools.partial(add_kernel, cols_blocks),
+        grid=(row_len // TOTAL,),
+        out_shape=jax.ShapeDtypeStruct((row_len, col_len), jnp.float32),
+        in_specs=[smem, smem, wide, pl.BlockSpec(memory_space=pltpu.VMEM)],
+        out_specs=wide,
+        scratch_shapes=[pltpu.SMEM((codes.shape[0],), jnp.int32)],
+        input_output_aliases={2: 0},
+        compiler_params=pltpu.CompilerParams(vmem_limit_bytes=40 * MIB),
+    )(codes, place, partial, arrived)
 
 
 def panel_kernel(code_ref, first_ref, front_ref, arrived_ref, out_ref):
@@ -166,8 +315,8 @@
     step = pl.program_id(0)
     sources, capacity = code_ref.shape
     height, width = front_ref.shape
-    side = arrived_ref.shape[1]
-    per_step = height // side
+    unit, side = arrived_ref.shape[2:]
+    per_step = height // unit
 
     @pl.when(step == 0)
     def _():
@@ -192,11 +341,11 @@
 
         def add(k):
             code = code_ref[s, k]
-            block_row = code // cols_blocks - step * per_step
+            unit_row = code // cols_blocks - step * per_step
             block_col = code % cols_blocks
-            rows = pl.ds(pl.multiple_of(block_row * side, side), side)
+            rows = pl.ds(pl.multiple_of(unit_row * unit, unit), unit)
             columns = pl.ds(pl.multiple_of(block_col * side, side), side)
-            out_ref[rows, columns] += arrived_ref[s * capacity + k]
+            out_ref[rows, columns] += arrived_ref[s, k]
             return k + 1
 
         cursor[s] = lax.while_loop(more, add, cursor[s])
@@ -301,32 +450,117 @@
     by_shift = (row_now - jnp.arange(row_count)) % row_count
     panel_codes = jnp.take(panel_codes, by_shift, axis=0).reshape(-1)
 
-    order = (target * rows_blocks * cols_blocks + code) * per_device + position
-    ranking = jnp.sum(
-        (target[:, :, None] == target[:, None, :]) & (order[:, None, :] < order[:, :, None]), axis=2
-    )
-    slot = own(target) * capacity + own(ranking)
-    here = (target == device_now)[:, :, None] & (ranking[:, :, None] == slots)
-    codes = jnp.sum(jnp.where(here, code[:, :, None] + 1, 0), axis=1) - 1
-    outgoing = pack(tiles, slot, valid_rows, device_count * capacity)
-    outgoing, *panel_in = lax.optimization_barrier((outgoing, *panel_in))
-    arrived = lax.all_to_all(
-        outgoing.reshape(device_count, capacity, side, side), ("row", "col"), 0, 0, tiled=True
-    ).reshape(device_count * capacity, side, side)
+    units = side // UNIT
+    length = capacity * units
+    width = length * 9 // 16
+    pass_on = length * 3 // 8
+    half_count = device_count // 2
+    half_base = device_now // half_count * half_count
+    unit_rows = rows_blocks * units
+    local_codes = unit_rows * cols_blocks
+    own_target, own_code = own(target), own(code)
+    own_position = own(position)
+    filled = (valid_rows + UNIT - 1) // UNIT
+    key = (own_target * rows_blocks * cols_blocks + own_code) * per_device + own_position
+    before = key[None, :] < key[:, None]
+    together = own_target[None, :] == own_target[:, None]
+    base = jnp.sum(jnp.where(before & together, filled[None, :], 0), axis=1)
+    order = jnp.sum(before, axis=1)
+    unit_code = (own_target * unit_rows + own_code // cols_blocks * units) * cols_blocks
+    unit_code += own_code % cols_blocks
+    meta = jnp.stack([own_position, own_target, base, filled, unit_code, valid_rows])
+    meta = jnp.sum(
+        jnp.where(order[None, :, None] == jnp.arange(per_device), meta[:, :, None], 0), axis=1
+    )
+    to_device = own_target[:, None] == jnp.arange(device_count)
+    load = jnp.sum(jnp.where(to_device, filled[:, None], 0), axis=0).reshape(2, half_count)
+    empty = load == 0
+    empty_rank = jnp.cumsum(empty, axis=1) - 1
+    device_ids = jnp.arange(device_count).reshape(2, half_count)
+    listed = (empty[:, :, None]) & (empty_rank[:, :, None] == jnp.arange(half_count))
+    empties = jnp.sum(jnp.where(listed, device_ids[:, :, None], 0), axis=1)
+    free = jnp.sum(empty, axis=1)
+    left = jnp.sum(jnp.maximum(load - width, 0), axis=1)
+    failed = jnp.any(left > free * width)
+    counts = jnp.concatenate([jnp.sum(own_target < half_count)[None], free]).astype(jnp.int32)
+    outgoing, sent_codes = spread(
+        tiles, meta.astype(jnp.int32), empties.astype(jnp.int32), counts,
+        device_count, width, length, cols_blocks,
+    )
+
+    got = lax.all_to_all(sent_codes[:, :width], ("row", "col"), 0, 0, tiled=True)
+    got_target = got // local_codes
+    local = got % local_codes
+    mine = (got >= 0) & (got_target == device_now)
+    direct_codes = jnp.where(mine, local, -1)
+    total_units = device_count * width
+    passing = ((got >= 0) & (got_target != device_now)).reshape(-1)
+    flat_key = jnp.where(passing, got.reshape(-1) * total_units + jnp.arange(total_units), -1)
+    flat_target = jnp.where(passing, got_target.reshape(-1), -1)
+    rank = jnp.sum(
+        (flat_target[None, :] == flat_target[:, None]) & (flat_key[None, :] < flat_key[:, None]), axis=1
+    )
+    failed = failed | jnp.any(passing & (rank >= pass_on))
+    relay_slot = jnp.where(
+        passing & (rank < pass_on), (flat_target - half_base) * pass_on + rank, -1
+    )
+    picked = relay_slot[:, None] == jnp.arange(half_count * pass_on)
+    relay_codes = jnp.sum(jnp.where(picked, local.reshape(-1)[:, None] + 1, 0), axis=0) - 1
+    notes = jnp.zeros((2, half_count, pass_on + 1), jnp.int32)
+    notes = lax.dynamic_update_slice(
+        notes, relay_codes.reshape(1, half_count, pass_on).astype(jnp.int32), (device_now // half_count, 0, 0)
+    )
+    notes = notes.at[:, :, pass_on].set(failed.astype(jnp.int32))
+    notes = lax.all_to_all(
+        notes.reshape(device_count, pass_on + 1), ("row", "col"), 0, 0, tiled=True
+    )
+    too_full = jnp.any(notes[:, pass_on] != 0)
+    relay_codes = lax.dynamic_slice_in_dim(notes, half_base, half_count, 0)[:, :pass_on]
+    relay_slot = relay_slot.reshape(device_count, width)
 
     first = (col_now == 0).astype(jnp.int32).reshape(1)
     partial = raw_panel(front, jnp.concatenate(panel_in, 0), panel_codes, first)
     raw_rows = lax.psum(partial, "col")
     slice_start = col_now * col_len % row_len
     slice_root = col_now * col_len // row_len
-    picked = lax.dynamic_slice_in_dim(raw_rows, slice_start, col_len, 0)
-    raw_cols = lax.psum(jnp.where(row_now == slice_root, picked, 0.0), "row")
-    diagonal = jnp.where(row_now == 0, raw_rows[:TOTAL], jnp.eye(TOTAL, dtype=jnp.float32))
-    lower, inverse = factor(diagonal)
-    inverse = lax.psum(jnp.where(row_now == 0, inverse, 0.0), "row")
-    rows = solve_rows(raw_rows, inverse)
-    cols = solve_cols(raw_cols, inverse)
-    return finish(front, rows, cols, lower, arrived, codes, place, cols_blocks)
+
+    def chain(raw_rows):
+        picked = lax.dynamic_slice_in_dim(raw_rows, slice_start, col_len, 0)
+        raw_cols = lax.psum(jnp.where(row_now == slice_root, picked, 0.0), "row")
+        diagonal = jnp.where(row_now == 0, raw_rows[:TOTAL], jnp.eye(TOTAL, dtype=jnp.float32))
+        lower, inverse = factor(diagonal)
+        inverse, raw_cols = lax.optimization_barrier((inverse, raw_cols))
+        inverse = lax.psum(jnp.where(row_now == 0, inverse, 0.0), "row")
+        return solve_rows(raw_rows, inverse), solve_cols(raw_cols, inverse), lower
+
+    def relayed(front, tiles, valid_rows, outgoing, raw_rows):
+        arrived = lax.all_to_all(outgoing, ("row", "col"), 0, 0, tiled=True)
+        rows, cols, lower = chain(raw_rows)
+        passed = relay(relay_slot, arrived, half_count * pass_on)
+        halves = [list(range(half_count)), list(range(half_count, device_count))]
+        passed = lax.all_to_all(
+            passed.reshape(half_count, pass_on, UNIT, side), ("row", "col"), 0, 0,
+            axis_index_groups=halves, tiled=True,
+        )
+        partial = finish(front, rows, cols, lower, arrived, direct_codes, place, cols_blocks)
+        return add_relayed(partial, passed, relay_codes, place, cols_blocks)
+
+    def padded(front, tiles, valid_rows, outgoing, raw_rows):
+        order = (target * rows_blocks * cols_blocks + code) * per_device + position
+        ranking = jnp.sum(
+            (target[:, :, None] == target[:, None, :]) & (order[:, None, :] < order[:, :, None]), axis=2
+        )
+        slot = own(target) * capacity + own(ranking)
+        here = (target == device_now)[:, :, None] & (ranking[:, :, None] == slots)
+        codes = jnp.sum(jnp.where(here, code[:, :, None] + 1, 0), axis=1) - 1
+        packed = pack(tiles, slot, valid_rows, device_count * capacity)
+        arrived = lax.all_to_all(
+            packed.reshape(device_count, capacity, side, side), ("row", "col"), 0, 0, tiled=True
+        )
+        rows, cols, lower = chain(raw_rows)
+        return finish(front, rows, cols, lower, arrived, codes, place, cols_blocks)
+
+    return lax.cond(too_full, padded, relayed, front, tiles, valid_rows, outgoing, raw_rows)
 
 
 def solution(mesh):

time: 601 us -> 703 us (1.17)
  the two profiles are of different devices: /device:TPU:0 before, /device:TPU:7 now
where the time goes in v3:
time: 703 us; the launch traced here: 695 us
  waiting for transfers between devices  436 us (62%)
  Pallas kernels  111 us (16%)
  other arithmetic  71.9 us (10%)
  local copies, waits for them, and re-layouts  25 us (4%)
  starting transfers between devices  23 us (3%)
  between operations  15.7 us (2%)
  loops' own time  10.1 us (1%)
    psum x1, waiting for transfers between devices, chain(): raw_cols = lax.psum(jnp.where(row_now == slice_root, picked, 0.0), 'row')  154 us
    all_to_all x1, waiting for transfers between devices, padded(): lax.all_to_all(packed.reshape(device_count, capacity, side, side), ('row'...  134 us
    psum x1, waiting for transfers between devices, chain(): inverse = lax.psum(jnp.where(row_now == 0, inverse, 0.0), 'row')  76.3 us
    psum x1, waiting for transfers between devices, body(): raw_rows = lax.psum(partial, 'col')  58.2 us
    pallas_call x1, Pallas kernels, finish(): pl.pallas_call(functools.partial(final_kernel, cols_blocks), grid=(row_le...  45.3 us
    pallas_call x2, Pallas kernels, pack(): pl.pallas_call(pack_kernel, out_shape=jax.ShapeDtypeStruct((n_slots, side...  26.6 us
    pallas_call x1, Pallas kernels, spread(): pl.pallas_call(functools.partial(spread_kernel, width, stride), out_shape...  25.7 us
    another operation x6, other arithmetic, lower_of(): return jnp.linalg.cholesky(jnp.tril(block) + jnp.tril(block, -1).T)  24.9 us
  transfers between devices with their start and end apart: 9, of which 6 were waited for; matrix products, arithmetic and copies ran while one was open for 10% of the time, Pallas kernels for 5%

profile of v3, /device:TPU:7, one launch (start us, length us, event | category | flops | bytes accessed | tf_op | source)
XLA Modules:
  0.0 694.9 jit_solution(4013551446951011875)
XLA Ops:
  9.4 7.7 %shard_map.49 = f32[32,128,128]{2,1,0:T(8,128)S(1)} custom-call(s32[128]{0:T(128)S(1)} %get-tuple-element.302.slot_ref, s32[128]{0:T(128)} %valid_ref.1, f32[128,128,128]{2,1,0:T(8,128)} %tiles_ref.1), custom_call_target="tpu_custom_call" | custom-call | tf_op jit(solution)/shard_map/pallas_call | solution.py:53
  17.2 3.6 collective-permute-start.2
  23.1 25.7 %shard_map.48 = (f32[32,72,8,128]{3,2,1,0:T(8,128)}, s32[32,128]{1,0:T(8,128)}) custom-call(s32[6,128]{1,0:T(8,128)S(1)} %select_reduce_fusion.6.meta_ref, s32[2,16]{1,0:T(2,128)S(1)} %select_reduce_fusion.9.empty_ref, s32[3]{0:T(128)S(1)} %pad_add_fusion.count_ref, f32[128,16,8,128]{3,2,1,0:T(8,128)} %bitcast.132), custom_call_target="tpu_custom_call" | custom-call | tf_op jit(solution)/shard_map/pallas_call | solution.py:118
  48.8 6.5 all-to-all-start.3
  57.9 8.4 %all-to-all-done.3 = s32[32,1,72]{2,1,0:T(1,128)S(1)} async-done(((s32[32,1,72]{2,1,0:T(1,128)}), s32[32,1,72]{2,1,0:T(1,128)S(1)}, u32[]{:S(2)}, u32[]{:S(2)}) %all-to-all-start.3) | async-done | bytes 9248 | tf_op jit(solution)/shard_map/all_to_all | solution.py:491
  68.9 3.3 shard_map.50
  72.1 2.0 copy-done.1
  74.2 4.4 convert_reduce_fusion.1
  80.5 1.3 select_reduce_fusion.5
  83.9 1.5 scatter.4
  85.3 6.4 all-to-all-start.4
  91.7 4.8 all-to-all-done.4
  97.7 58.2 %all-reduce.18.cloned.1.call-done = f32[4096,256]{1,0:T(8,128)} async-done(((f32[4096,256]{1,0:T(8,128)}), f32[4096,256]{1,0:T(8,128)}) %all-reduce.18.cloned.1.call-update) | async-done | bytes 4194320 | tf_op jit(solution)/shard_map/psum | solution.py:523
  157.0 530.8 %conditional.1 = (f32[4096,2048]{1,0:T(8,128)}) conditional(s32[]{:T(128)} %convert_element_type.54, (s32[]{:T(128)}, s32[32,1,49]{2,1,0:T(1,128)}, s32[32,72]{1,0:T(8,128)S(1)}, s32[32,72]{1,0:T(8,128)S(1)}, pred[32,72]{1,0:T(8,128)(4,1)S(1)}, /*index=5*/pred[32,72]{1,0:T(8,128)(4,1)S(1)}, s32[32,72]{1,0:T(8,128)S(1)}, s32[]{:T(128)}, s32[]{:T(128)}, ...), branch_computations={%region_17.24_spmd, %region_22.29_spmd} | conditional | flops 156226176 | bytes 201392864 | solution.py:563
  167.3 3.0 convert_reduce_fusion
  171.0 18.9 %branch_1_fun.6 = f32[256,128,128]{2,1,0:T(8,128)S(1)} custom-call(s32[128]{0:T(128)S(1)} %fusion.28.slot_ref, s32[128]{0:T(128)} %get-tuple-element.196.valid_ref, f32[128,128,128]{2,1,0:T(8,128)} %get-tuple-element.197.tiles_ref), custom_call_target="tpu_custom_call" | custom-call | tf_op jit(solution)/shard_map/cond/branch_1_fun/pallas_call | solution.py:53
  190.0 6.2 copy-done
  196.1 6.1 all-to-all-start.2
  202.3 3.1 dynamic-slice_select_fusion.1
  206.8 11.7 %cholesky.96 = f32[128,128]{1,0:T(8,128)S(1)} custom-call(f32[128,128]{1,0:T(8,128)S(1)} %copy.155), custom_call_target="Cholesky" | custom-call | tf_op jit(solution)/shard_map/cond/branch_1_fun/jit(cholesky)/cholesky | solution.py:388
  220.0 9.8 %custom-call.10 = f32[1,128,128]{1,2,0:T(8,128)S(1)} custom-call(f32[1,128,128]{2,1,0:T(8,128)S(1)} %get-tuple-element.277), custom_call_target="InvertDiagBlocksLowerTriangular" | custom-call | tf_op jit(solution)/shard_map/cond/branch_1_fun/jit(_solve_triangular)/triangular_solve | solution.py:391
  231.3 11.7 %cholesky.107 = f32[128,128]{1,0:T(8,128)S(1)} custom-call(f32[128,128]{1,0:T(8,128)S(1)} %fusion.22), custom_call_target="Cholesky" | custom-call | tf_op jit(solution)/shard_map/cond/branch_1_fun/jit(cholesky)/cholesky | solution.py:388
  244.4 10.0 %custom-call.11 = f32[1,128,128]{1,2,0:T(8,128)S(1)} custom-call(f32[1,128,128]{2,1,0:T(8,128)S(1)} %get-tuple-element.275), custom_call_target="InvertDiagBlocksLowerTriangular" | custom-call | tf_op jit(solution)/shard_map/cond/branch_1_fun/jit(_solve_triangular)/triangular_solve | solution.py:391
  256.2 154.5 %all-reduce.14.cloned.1.call-done.raw_ref = f32[2048,256]{1,0:T(8,128)} async-done(((f32[2048,256]{1,0:T(8,128)}), f32[2048,256]{1,0:T(8,128)}) %all-reduce.14.cloned.1.call-update) | async-done | bytes 2097168 | tf_op jit(solution)/shard_map/cond/branch_1_fun/psum | solution.py:529
  412.7 76.3 %all-reduce.16.cloned.1.call-done.inverse_ref = f32[256,256]{1,0:T(8,128)} async-done(((f32[256,256]{1,0:T(8,128)}), f32[256,256]{1,0:T(8,128)}) %all-reduce.16.cloned.1.call-update) | async-done | bytes 262160 | tf_op jit(solution)/shard_map/cond/branch_1_fun/psum | solution.py:533
  490.0 7.4 %branch_1_fun.4 = (f32[4096,256]{1,0:T(8,128)S(1)}, bf16[4096,256]{1,0:T(8,128)(2,1)S(1)}, bf16[4096,256]{1,0:T(8,128)(2,1)S(1)}) custom-call(f32[4096,256]{1,0:T(8,128)} %get-tuple-element.184.raw_ref, f32[256,256]{1,0:T(8,128)S(1)} %copy-done.17), custom_call_target="tpu_custom_call" | custom-call | tf_op jit(solution)/shard_map/cond/branch_1_fun/pallas_call | solution.py:270
  497.5 1.9 copy-done.3
  499.4 1.4 copy-done.5
  500.8 1.3 copy-done.6
  502.1 2.8 branch_1_fun.5
  508.2 134.1 %all-to-all-done.2.arrived_ref = f32[32,8,128,128]{3,2,1,0:T(8,128)} async-done(((f32[32,8,128,128]{3,2,1,0:T(8,128)}), f32[32,8,128,128]{3,2,1,0:T(8,128)}, u32[]{:S(2)}, u32[]{:S(2)}) %all-to-all-start.2) | async-done | bytes 16777248 | tf_op jit(solution)/shard_map/cond/branch_1_fun/all_to_all | solution.py:557
  642.3 45.3 %branch_1_fun.7 = f32[4096,2048]{1,0:T(8,128)} custom-call(s32[32,8]{1,0:T(8,128)} %broadcast_add_fusion.code_ref, s32[2]{0:T(128)S(1)} %copy-done.26, f32[4096,2048]{1,0:T(8,128)} %get-tuple-element.183.front_ref, f32[4096,256]{1,0:T(8,128)} %copy-done.3, bf16[4096,256]{1,0:T(8,128)(2,1)} %copy-done.5, bf16[4096,256]{1,0:T(8,128)(2,1)} %copy-done.6, ...), custom_call_target="tpu_custom_call" | custom-call | tf_op jit(solution)/shard_map/cond/branch_1_fun/pallas_call | solution.py:371
  (138 shorter events, 29.8 us)
Async XLA Ops:
  7.4 1.9 copy-start.19
  17.1 4.1 copy-start.24
  17.2 50.4 %collective-permute-start.2 = (f32[8,128,128]{2,1,0:T(8,128)S(1)}, f32[8,128,128]{2,1,0:T(8,128)S(1)}, u32[]{:S(2)}, u32[]{:S(2)}) collective-permute-start(f32[8,128,128]{2,1,0:T(8,128)S(1)} %get-tuple-element.286), channel_id=1, source_target_pairs={{0,24},{8,0},{16,8},{24,16},{1,25},{9,1},{17,9},{25,17},{2,26},{10... | collective-permute-start | bytes 1572872 | tf_op jit(solution)/shard_map/ppermute | solution.py:441
  20.8 46.9 %collective-permute-start.1 = (f32[8,128,128]{2,1,0:T(8,128)S(1)}, f32[8,128,128]{2,1,0:T(8,128)S(1)}, u32[]{:S(2)}, u32[]{:S(2)}) collective-permute-start(f32[8,128,128]{2,1,0:T(8,128)S(1)} %get-tuple-element.287), channel_id=1, source_target_pairs={{0,16},{8,24},{16,0},{24,8},{1,17},{9,25},{17,1},{25,9},{2,18},{10... | collective-permute-start | bytes 1572872 | tf_op jit(solution)/shard_map/ppermute | solution.py:441
  20.8 46.9 %collective-permute-start = (f32[8,128,128]{2,1,0:T(8,128)S(1)}, f32[8,128,128]{2,1,0:T(8,128)}, u32[]{:S(2)}, u32[]{:S(2)}) collective-permute-start(f32[8,128,128]{2,1,0:T(8,128)S(1)} %get-tuple-element.288), channel_id=1, source_target_pairs={{0,8},{8,16},{16,24},{24,0},{1,9},{9,17},{17,25},{25,1},{2,10},{10... | collective-permute-start | bytes 1572872 | tf_op jit(solution)/shard_map/ppermute | solution.py:441
  48.8 17.5 %all-to-all-start.3 = ((s32[32,1,72]{2,1,0:T(1,128)}), s32[32,1,72]{2,1,0:T(1,128)S(1)}, u32[]{:S(2)}, u32[]{:S(2)}) async-start(s32[32,1,72]{2,1,0:T(1,128)} %bitcast.33), calls=%async_computation.3 | async-start | bytes 32768 | tf_op jit(solution)/shard_map/all_to_all | solution.py:491
  55.4 100.5 %all-reduce.18.cloned.1.call-start = ((), (), s32[]{:S(2)}) async-start(), calls=%async_computation.9 | async-start | bytes 8388608 | tf_op jit(solution)/shard_map/psum | solution.py:523
  72.1 2.0 copy-start.1
  85.3 11.1 %all-to-all-start.4 = ((s32[32,1,49]{2,1,0:T(1,128)}), s32[32,1,49]{2,1,0:T(1,128)S(1)}, u32[]{:S(2)}, u32[]{:S(2)}) async-start(s32[32,1,49]{2,1,0:T(1,128)} %bitcast.39), calls=%async_computation.4 | async-start | bytes 32768 | tf_op jit(solution)/shard_map/all_to_all | solution.py:514
  96.5 60.6 %copy-start.23 = (s32[32,1,49]{2,1,0:T(1,128)}, s32[32,1,49]{2,1,0:T(1,128)S(1)}, u32[]{:S(2)}) copy-start(s32[32,1,49]{2,1,0:T(1,128)S(1)} %all-to-all-done.4) | copy-start | bytes 18820
  190.0 6.2 copy-start
  196.1 446.2 %all-to-all-start.2 = ((f32[32,8,128,128]{3,2,1,0:T(8,128)}), f32[32,8,128,128]{3,2,1,0:T(8,128)}, u32[]{:S(2)}, u32[]{:S(2)}) async-start(f32[32,8,128,128]{3,2,1,0:T(8,128)} %bitcast.129), calls=%async_computation.2 | async-start | bytes 33554432 | tf_op jit(solution)/shard_map/cond/branch_1_fun/all_to_all | solution.py:557
  202.2 208.5 %all-reduce.14.cloned.1.call-start = ((), (), s32[]{:S(2)}) async-start(), calls=%async_computation.7 | async-start | bytes 4194304 | tf_op jit(solution)/shard_map/cond/branch_1_fun/psum | solution.py:529
  205.4 283.7 %all-reduce.16.cloned.1.call-start = ((), (), s32[]{:S(2)}) async-start(), calls=%async_computation.8 | async-start | bytes 524288 | tf_op jit(solution)/shard_map/cond/branch_1_fun/psum | solution.py:533
  206.6 49.6 %copy-start.20 = (s32[32,128]{1,0:T(8,128)S(1)}, s32[32,128]{1,0:T(8,128)}, u32[]{:S(2)}) copy-start(s32[32,128]{1,0:T(8,128)} %get-tuple-element.177) | copy-start | bytes 49156 | tf_op jit(solution)/shard_map/cond
  220.0 191.5 %copy-start.28 = (s32[8]{0:T(128)S(1)}, s32[8]{0:T(128)}, u32[]{:S(2)}) copy-start(s32[8]{0:T(128)} %get-tuple-element.181) | copy-start | bytes 100 | tf_op jit(solution)/shard_map/cond
  412.7 89.4 %copy-start.12 = (f32[2048,256]{1,0:T(8,128)S(1)}, f32[2048,256]{1,0:T(8,128)}, u32[]{:S(2)}) copy-start(f32[2048,256]{1,0:T(8,128)} %all-reduce.14.cloned.1.call-done.raw_ref) | copy-start | bytes 6291460 | tf_op jit(solution)/shard_map/cond
  489.1 0.9 copy-start.17
  497.5 2.0 copy-start.3
  499.4 1.4 copy-start.5
  500.8 1.3 copy-start.6
  502.1 140.2 %copy-start.26 = (s32[2]{0:T(128)S(1)}, s32[2]{0:T(128)}, u32[]{:S(2)}) copy-start(s32[2]{0:T(128)} %get-tuple-element.182.place_ref) | copy-start | bytes 28 | tf_op jit(solution)/shard_map/cond
  505.0 1.3 copy-start.7
  506.3 1.0 copy-start.13
  507.3 1.0 copy-start.14
Sparse Core Ops, SparseCore 0:
  74.3 81.5 all-reduce.17
  205.5 205.1 all-reduce.13
  413.1 75.8 all-reduce.15

commit v4 on v3

--- a/solution.py
+++ b/solution.py
@@ -452,7 +452,7 @@
 
     units = side // UNIT
     length = capacity * units
-    width = length * 9 // 16
+    width = length * 21 // 32
     pass_on = length * 3 // 8
     half_count = device_count // 2
     half_base = device_now // half_count * half_count

time: 703 us -> 727 us (1.034)
  the two profiles are of different devices: /device:TPU:7 before, /device:TPU:15 now
where the time goes in v4:
time: 727 us; the launch traced here: 719 us
  waiting for transfers between devices  387 us (53%)
  Pallas kernels  169 us (23%)
  other arithmetic  77.2 us (11%)
  starting transfers between devices  35.9 us (5%)
  local copies, waits for them, and re-layouts  27.9 us (4%)
  between operations  15.7 us (2%)
    all_to_all x1, waiting for transfers between devices, relayed(): arrived = lax.all_to_all(outgoing, ('row', 'col'), 0, 0, tiled=True)  236 us
    pallas_call x1, Pallas kernels, finish(): pl.pallas_call(functools.partial(final_kernel, cols_blocks), grid=(row_le...  79.8 us
    psum x1, waiting for transfers between devices, body(): raw_rows = lax.psum(partial, 'col')  57.2 us
    psum x1, waiting for transfers between devices, chain(): raw_cols = lax.psum(jnp.where(row_now == slice_root, picked, 0.0), 'row')  45.8 us
    pallas_call x1, Pallas kernels, add_relayed(): pl.pallas_call(functools.partial(add_kernel, cols_blocks), grid=(row_len...  36.5 us
    psum x1, waiting for transfers between devices, chain(): inverse = lax.psum(jnp.where(row_now == 0, inverse, 0.0), 'row')  34.1 us
    another operation x6, other arithmetic, lower_of(): return jnp.linalg.cholesky(jnp.tril(block) + jnp.tril(block, -1).T)  25.7 us
    pallas_call x1, Pallas kernels, spread(): pl.pallas_call(functools.partial(spread_kernel, width, stride), out_shape...  23.4 us
  transfers between devices with their start and end apart: 10, of which 6 were waited for; matrix products, arithmetic and copies ran while one was open for 12% of the time, Pallas kernels for 16%

profile of v4, /device:TPU:15, one launch (start us, length us, event | category | flops | bytes accessed | tf_op | source)
XLA Modules:
  0.0 719.4 jit_solution(6210284928928227122)
XLA Ops:
  9.4 7.9 %shard_map.49 = f32[32,128,128]{2,1,0:T(8,128)S(1)} custom-call(s32[128]{0:T(128)S(1)} %get-tuple-element.302.slot_ref, s32[128]{0:T(128)} %valid_ref.1, f32[128,128,128]{2,1,0:T(8,128)} %tiles_ref.1), custom_call_target="tpu_custom_call" | custom-call | tf_op jit(solution)/shard_map/pallas_call | solution.py:53
  17.7 2.0 collective-permute-start.1
  19.7 2.3 collective-permute-start
  24.0 23.4 %shard_map.48 = (f32[32,84,8,128]{3,2,1,0:T(8,128)}, s32[32,128]{1,0:T(8,128)}) custom-call(s32[6,128]{1,0:T(8,128)S(1)} %select_reduce_fusion.6.meta_ref, s32[2,16]{1,0:T(2,128)S(1)} %select_reduce_fusion.9.empty_ref, s32[3]{0:T(128)S(1)} %pad_add_fusion.count_ref, f32[128,16,8,128]{3,2,1,0:T(8,128)} %bitcast.132), custom_call_target="tpu_custom_call" | custom-call | tf_op jit(solution)/shard_map/pallas_call | solution.py:118
  47.4 5.6 all-to-all-start.3
  55.6 9.6 %all-to-all-done.3 = s32[32,1,84]{2,1,0:T(1,128)S(1)} async-done(((s32[32,1,84]{2,1,0:T(1,128)}), s32[32,1,84]{2,1,0:T(1,128)S(1)}, u32[]{:S(2)}, u32[]{:S(2)}) %all-to-all-start.3) | async-done | bytes 10784 | tf_op jit(solution)/shard_map/all_to_all | solution.py:491
  67.8 3.3 shard_map.50
  71.1 2.0 copy-done.1
  73.1 5.8 convert_reduce_fusion.1
  81.1 1.5 select_reduce_fusion.5
  86.1 7.4 %all-to-all-start.4 = ((s32[32,1,49]{2,1,0:T(1,128)}), s32[32,1,49]{2,1,0:T(1,128)S(1)}, u32[]{:S(2)}, u32[]{:S(2)}) async-start(s32[32,1,49]{2,1,0:T(1,128)} %bitcast.39), calls=%async_computation.4 | async-start | bytes 32768 | tf_op jit(solution)/shard_map/all_to_all | solution.py:514
  93.4 3.9 all-to-all-done.4
  98.7 57.2 %all-reduce.18.cloned.1.call-done = f32[4096,256]{1,0:T(8,128)} async-done(((f32[4096,256]{1,0:T(8,128)}), f32[4096,256]{1,0:T(8,128)}) %all-reduce.18.cloned.1.call-update) | async-done | bytes 4194320 | tf_op jit(solution)/shard_map/psum | solution.py:523
  157.0 555.6 %conditional.1 = (f32[4096,2048]{1,0:T(8,128)}) conditional(s32[]{:T(128)} %convert_element_type.54, (s32[]{:T(128)}, s32[32,1,49]{2,1,0:T(1,128)}, s32[32,84]{1,0:T(8,128)S(1)}, s32[32,84]{1,0:T(8,128)S(1)}, pred[32,84]{1,0:T(8,128)(4,1)S(1)}, /*index=5*/pred[32,84]{1,0:T(8,128)(4,1)S(1)}, s32[32,84]{1,0:T(8,128)S(1)}, s32[]{:T(128)}, s32[]{:T(128)}, ...), branch_computations={%region_17.24_spmd, %region_22.29_spmd} | conditional | flops 156226176 | bytes 201392864 | solution.py:563
  157.0 6.1 all-to-all-start
  163.8 236.3 %all-to-all-done.arrived_ref = f32[32,84,8,128]{3,2,1,0:T(8,128)} async-done(((f32[32,84,8,128]{3,2,1,0:T(8,128)}), f32[32,84,8,128]{3,2,1,0:T(8,128)}, u32[]{:S(2)}, u32[]{:S(2)}) %all-to-all-start) | async-done | bytes 11010080 | tf_op jit(solution)/shard_map/cond/branch_0_fun/all_to_all | solution.py:537
  400.1 7.2 %branch_0_fun.8 = f32[768,8,128]{2,1,0:T(8,128)S(1)} custom-call(s32[32,84]{1,0:T(8,128)S(1)} %get-tuple-element.269.slot_ref, f32[32,84,8,128]{3,2,1,0:T(8,128)} %all-to-all-done.arrived_ref), custom_call_target="tpu_custom_call" | custom-call | tf_op jit(solution)/shard_map/cond/branch_0_fun/pallas_call | solution.py:151
  407.3 1.6 copy-done.2
  408.9 12.1 %all-to-all-start.1 = ((f32[16,48,8,128]{3,2,1,0:T(8,128)}), f32[16,48,8,128]{3,2,1,0:T(8,128)S(1)}, u32[]{:S(2)}, u32[]{:S(2)}) async-start(f32[16,48,8,128]{3,2,1,0:T(8,128)} %bitcast.130), calls=%async_computation.1 | async-start | bytes 6291456 | tf_op jit(solution)/shard_map/cond/branch_0_fun/all_to_all | solution.py:541
  421.0 3.1 dynamic-slice_select_fusion
  428.4 12.6 %cholesky.74 = f32[128,128]{1,0:T(8,128)S(1)} custom-call(f32[128,128]{1,0:T(8,128)} %copy.143), custom_call_target="Cholesky" | custom-call | tf_op jit(solution)/shard_map/cond/branch_0_fun/jit(cholesky)/cholesky | solution.py:388
  442.8 9.8 %custom-call.8 = f32[1,128,128]{1,2,0:T(8,128)S(1)} custom-call(f32[1,128,128]{2,1,0:T(8,128)S(1)} %get-tuple-element.273), custom_call_target="InvertDiagBlocksLowerTriangular" | custom-call | tf_op jit(solution)/shard_map/cond/branch_0_fun/jit(_solve_triangular)/triangular_solve | solution.py:391
  461.5 11.7 %cholesky.85 = f32[128,128]{1,0:T(8,128)S(1)} custom-call(f32[128,128]{1,0:T(8,128)S(1)} %fusion.7), custom_call_target="Cholesky" | custom-call | tf_op jit(solution)/shard_map/cond/branch_0_fun/jit(cholesky)/cholesky | solution.py:388
  475.2 10.2 %custom-call.9 = f32[1,128,128]{1,2,0:T(8,128)S(1)} custom-call(f32[1,128,128]{2,1,0:T(8,128)S(1)} %get-tuple-element.271), custom_call_target="InvertDiagBlocksLowerTriangular" | custom-call | tf_op jit(solution)/shard_map/cond/branch_0_fun/jit(_solve_triangular)/triangular_solve | solution.py:391
  487.8 1.6 select_maximum_fusion.lower_ref
  489.4 45.8 %all-reduce.10.cloned.1.call-done.raw_ref = f32[2048,256]{1,0:T(8,128)} async-done(((f32[2048,256]{1,0:T(8,128)}), f32[2048,256]{1,0:T(8,128)}) %all-reduce.10.cloned.1.call-update) | async-done | bytes 2097168 | tf_op jit(solution)/shard_map/cond/branch_0_fun/psum | solution.py:529
  538.1 34.1 %all-reduce.12.cloned.1.call-done.inverse_ref = f32[256,256]{1,0:T(8,128)} async-done(((f32[256,256]{1,0:T(8,128)}), f32[256,256]{1,0:T(8,128)}) %all-reduce.12.cloned.1.call-update) | async-done | bytes 262160 | tf_op jit(solution)/shard_map/cond/branch_0_fun/psum | solution.py:533
  573.2 7.6 %branch_0_fun.5 = (f32[4096,256]{1,0:T(8,128)S(1)}, bf16[4096,256]{1,0:T(8,128)(2,1)S(1)}, bf16[4096,256]{1,0:T(8,128)(2,1)S(1)}) custom-call(f32[4096,256]{1,0:T(8,128)} %get-tuple-element.163.raw_ref, f32[256,256]{1,0:T(8,128)S(1)} %copy-done.18), custom_call_target="tpu_custom_call" | custom-call | tf_op jit(solution)/shard_map/cond/branch_0_fun/pallas_call | solution.py:270
  580.8 2.0 copy-done.4
  585.4 2.8 branch_0_fun.6
  591.6 79.8 %branch_0_fun.7.partial_ref = f32[4096,2048]{1,0:T(8,128)} custom-call(s32[32,84]{1,0:T(8,128)} %fusion.12.code_ref, s32[2]{0:T(128)S(1)} %copy-done.25, f32[4096,2048]{1,0:T(8,128)} %get-tuple-element.162.front_ref, f32[4096,256]{1,0:T(8,128)} %copy-done.4, bf16[4096,256]{1,0:T(8,128)(2,1)} %copy-done.8, bf16[4096,256]{1,0:T(8,128)(2,1)} %copy-done.9, ...), custom_call_target="tpu_custom_call" | custom-call | tf_op jit(solution)/shard_map/cond/branch_0_fun/pallas_call | solution.py:371
  671.4 36.5 %branch_0_fun.9 = f32[4096,2048]{1,0:T(8,128)} custom-call(s32[16,48]{1,0:T(8,128)S(1)} %bitcast.131, s32[2]{0:T(128)S(1)} %copy-done.25, f32[4096,2048]{1,0:T(8,128)} %branch_0_fun.7.partial_ref, f32[16,48,8,128]{3,2,1,0:T(8,128)S(1)} %all-to-all-done.1.arrived_ref), custom_call_target="tpu_custom_call", output_to_operand_aliasing={{}: (2, {})} | custom-call | tf_op jit(solution)/shard_map/cond/branch_0_fun/pallas_call | solution.py:202
  (141 shorter events, 46.0 us)
Async XLA Ops:
  7.4 1.9 copy-start.19
  17.3 4.7 copy-start.24
  17.5 49.1 %collective-permute-start.2 = (f32[8,128,128]{2,1,0:T(8,128)S(1)}, f32[8,128,128]{2,1,0:T(8,128)S(1)}, u32[]{:S(2)}, u32[]{:S(2)}) collective-permute-start(f32[8,128,128]{2,1,0:T(8,128)S(1)} %get-tuple-element.286), channel_id=1, source_target_pairs={{0,24},{8,0},{16,8},{24,16},{1,25},{9,1},{17,9},{25,17},{2,26},{10... | collective-permute-start | bytes 1572872 | tf_op jit(solution)/shard_map/ppermute | solution.py:441
  17.7 48.8 %collective-permute-start.1 = (f32[8,128,128]{2,1,0:T(8,128)S(1)}, f32[8,128,128]{2,1,0:T(8,128)S(1)}, u32[]{:S(2)}, u32[]{:S(2)}) collective-permute-start(f32[8,128,128]{2,1,0:T(8,128)S(1)} %get-tuple-element.287), channel_id=1, source_target_pairs={{0,16},{8,24},{16,0},{24,8},{1,17},{9,25},{17,1},{25,9},{2,18},{10... | collective-permute-start | bytes 1572872 | tf_op jit(solution)/shard_map/ppermute | solution.py:441
  19.7 46.8 %collective-permute-start = (f32[8,128,128]{2,1,0:T(8,128)S(1)}, f32[8,128,128]{2,1,0:T(8,128)}, u32[]{:S(2)}, u32[]{:S(2)}) collective-permute-start(f32[8,128,128]{2,1,0:T(8,128)S(1)} %get-tuple-element.288), channel_id=1, source_target_pairs={{0,8},{8,16},{16,24},{24,0},{1,9},{9,17},{17,25},{25,1},{2,10},{10... | collective-permute-start | bytes 1572872 | tf_op jit(solution)/shard_map/ppermute | solution.py:441
  47.4 17.8 %all-to-all-start.3 = ((s32[32,1,84]{2,1,0:T(1,128)}), s32[32,1,84]{2,1,0:T(1,128)S(1)}, u32[]{:S(2)}, u32[]{:S(2)}) async-start(s32[32,1,84]{2,1,0:T(1,128)} %bitcast.33), calls=%async_computation.3 | async-start | bytes 32768 | tf_op jit(solution)/shard_map/all_to_all | solution.py:491
  53.0 102.9 %all-reduce.18.cloned.1.call-start = ((), (), s32[]{:S(2)}) async-start(), calls=%async_computation.9 | async-start | bytes 8388608 | tf_op jit(solution)/shard_map/psum | solution.py:523
  71.1 2.0 copy-start.1
  86.1 11.2 %all-to-all-start.4 = ((s32[32,1,49]{2,1,0:T(1,128)}), s32[32,1,49]{2,1,0:T(1,128)S(1)}, u32[]{:S(2)}, u32[]{:S(2)}) async-start(s32[32,1,49]{2,1,0:T(1,128)} %bitcast.39), calls=%async_computation.4 | async-start | bytes 32768 | tf_op jit(solution)/shard_map/all_to_all | solution.py:514
  97.3 59.6 %copy-start.23 = (s32[32,1,49]{2,1,0:T(1,128)}, s32[32,1,49]{2,1,0:T(1,128)S(1)}, u32[]{:S(2)}) copy-start(s32[32,1,49]{2,1,0:T(1,128)S(1)} %all-to-all-done.4) | copy-start | bytes 18820
  157.0 6.2 copy-start.21
  157.0 6.2 copy-start.22
  157.0 243.1 %all-to-all-start = ((f32[32,84,8,128]{3,2,1,0:T(8,128)}), f32[32,84,8,128]{3,2,1,0:T(8,128)}, u32[]{:S(2)}, u32[]{:S(2)}) async-start(f32[32,84,8,128]{3,2,1,0:T(8,128)} %get-tuple-element.175), calls=%async_computation | async-start | bytes 22020096 | tf_op jit(solution)/shard_map/cond/branch_0_fun/all_to_all | solution.py:537
  407.3 1.6 copy-start.2
  408.9 262.5 %all-to-all-start.1 = ((f32[16,48,8,128]{3,2,1,0:T(8,128)}), f32[16,48,8,128]{3,2,1,0:T(8,128)S(1)}, u32[]{:S(2)}, u32[]{:S(2)}) async-start(f32[16,48,8,128]{3,2,1,0:T(8,128)} %bitcast.130), calls=%async_computation.1 | async-start | bytes 6291456 | tf_op jit(solution)/shard_map/cond/branch_0_fun/all_to_all | solution.py:541
  421.0 114.3 %all-reduce.10.cloned.1.call-start = ((), (), s32[]{:S(2)}) async-start(), calls=%async_computation.5 | async-start | bytes 4194304 | tf_op jit(solution)/shard_map/cond/branch_0_fun/psum | solution.py:529
  424.2 148.0 %all-reduce.12.cloned.1.call-start = ((), (), s32[]{:S(2)}) async-start(), calls=%async_computation.6 | async-start | bytes 524288 | tf_op jit(solution)/shard_map/cond/branch_0_fun/psum | solution.py:533
  425.6 0.6 copy-start.27
  572.2 0.9 copy-start.18
  573.2 12.3 %copy-start.11 = (f32[2048,256]{1,0:T(8,128)S(1)}, f32[2048,256]{1,0:T(8,128)}, u32[]{:S(2)}) copy-start(f32[2048,256]{1,0:T(8,128)} %all-reduce.10.cloned.1.call-done.raw_ref) | copy-start | bytes 6291460 | tf_op jit(solution)/shard_map/cond
  580.8 2.0 copy-start.4
  582.8 1.3 copy-start.8
  584.1 1.3 copy-start.9
  585.4 6.2 copy-start.25
  588.3 1.3 copy-start.10
  589.6 1.0 copy-start.15
  590.6 1.1 copy-start.16
Sparse Core Ops, SparseCore 0:
  73.2 82.5 all-reduce.17
  424.3 110.8 all-reduce.9
  537.7 34.4 all-reduce.11

commit v5 on v4

--- a/solution.py
+++ b/solution.py
@@ -157,58 +157,90 @@
     )(slots, arrived)
 
 
-def add_kernel(cols_blocks, code_ref, place_ref, partial_ref, arrived_ref, out_ref, cursor):
-    step = pl.program_id(0)
-    sources, capacity = code_ref.shape
-    unit, side = arrived_ref.shape[2:]
-    per_step = partial_ref.shape[0] // unit
-
-    @pl.when(step == 0)
-    def _():
-        for s in range(sources):
-            cursor[s] = 0
-
-    out_ref[...] = partial_ref[...]
-    edge = (step + 1) * per_step * cols_blocks
-
-    @pl.loop(0, sources)
-    def _(s):
-        def more(k):
-            code = code_ref[s, jnp.minimum(k, capacity - 1)]
-            return (k < capacity) & (code >= 0) & (code < edge)
-
-        def add(k):
-            code = code_ref[s, k]
-            unit_row = code // cols_blocks - step * per_step
-            block_col = code % cols_blocks
-            fixed = (place_ref[0] == 0) & (step == 0)
-            fixed |= (place_ref[1] == 0) & (block_col < PANELS)
-
-            @pl.when(jnp.logical_not(fixed))
+def add_kernel(
+    cols_blocks, block_ref, unit_ref, index_ref, count_ref, partial_ref, arrived_ref, out_ref, buf,
+    group_start, sem_in, sem_out
+):
+    slots, side = buf.shape[0], buf.shape[1]
+    unit = arrived_ref.shape[1]
+    ahead = slots // 2
+    count = count_ref[0]
+
+    def listed(i, carry):
+        groups, last = carry
+        block = block_ref[i]
+        fresh = block != last
+
+        @pl.when(fresh)
+        def _():
+            group_start[groups] = i
+
+        return jnp.where(fresh, groups + 1, groups), block
+
+    groups, _ = lax.fori_loop(0, count, listed, (jnp.int32(0), jnp.int32(-1)))
+    group_start[groups] = count
+
+    def window(g):
+        block = block_ref[group_start[g]]
+        rows = pl.ds(pl.multiple_of(block // cols_blocks * side, side), side)
+        columns = pl.ds(pl.multiple_of(block % cols_blocks * side, side), side)
+        return out_ref.at[rows, columns]
+
+    def fetch(g):
+        at = g % slots
+        return pltpu.make_async_copy(window(g), buf.at[at], sem_in.at[at])
+
+    def store(g):
+        at = g % slots
+        return pltpu.make_async_copy(buf.at[at], window(g), sem_out.at[at])
+
+    @pl.loop(0, jnp.minimum(groups, ahead))
+    def _(g):
+        fetch(g).start()
+
+    @pl.loop(0, groups)
+    def _(g):
+        @pl.when(g + ahead < groups)
+        def _():
+            @pl.when(g >= ahead)
             def _():
-                rows = pl.ds(pl.multiple_of(unit_row * unit, unit), unit)
-                columns = pl.ds(pl.multiple_of(block_col * side, side), side)
-                out_ref[rows, columns] += arrived_ref[s, k]
-
-            return k + 1
-
-        cursor[s] = lax.while_loop(more, add, cursor[s])
-
-
-def add_relayed(partial, arrived, codes, place, cols_blocks):
+                store(g - ahead).wait()
+
+            fetch(g + ahead).start()
+
+        fetch(g).wait()
+
+        @pl.loop(group_start[g], group_start[g + 1])
+        def _(i):
+            rows = pl.ds(pl.multiple_of(unit_ref[i] * unit, unit), unit)
+            buf[g % slots, rows] += arrived_ref[index_ref[i]]
+
+        store(g).start()
+
+    @pl.loop(jnp.maximum(groups - slots, 0), groups)
+    def _(g):
+        store(g).wait()
+
+
+def add_relayed(partial, arrived, listing, cols_blocks):
     row_len, col_len = partial.shape
+    unit, side = arrived.shape[1:]
     smem = pl.BlockSpec(memory_space=pltpu.SMEM)
-    wide = pl.BlockSpec((TOTAL, col_len), lambda i: (i, 0))
+    hbm = pl.BlockSpec(memory_space=pl.ANY)
     return pl.pallas_call(
         functools.partial(add_kernel, cols_blocks),
-        grid=(row_len // TOTAL,),
         out_shape=jax.ShapeDtypeStruct((row_len, col_len), jnp.float32),
-        in_specs=[smem, smem, wide, pl.BlockSpec(memory_space=pltpu.VMEM)],
-        out_specs=wide,
-        scratch_shapes=[pltpu.SMEM((codes.shape[0],), jnp.int32)],
-        input_output_aliases={2: 0},
-        compiler_params=pltpu.CompilerParams(vmem_limit_bytes=40 * MIB),
-    )(codes, place, partial, arrived)
+        in_specs=[smem, smem, smem, smem, hbm, pl.BlockSpec(memory_space=pltpu.VMEM)],
+        out_specs=hbm,
+        scratch_shapes=[
+            pltpu.VMEM((16, side, side), jnp.float32),
+            pltpu.SMEM((arrived.shape[0] + 1,), jnp.int32),
+            pltpu.SemaphoreType.DMA((16,)),
+            pltpu.SemaphoreType.DMA((16,)),
+        ],
+        input_output_aliases={4: 0},
+        compiler_params=pltpu.CompilerParams(vmem_limit_bytes=24 * MIB),
+    )(*listing, partial, arrived)
 
 
 def panel_kernel(code_ref, first_ref, front_ref, arrived_ref, out_ref):
@@ -257,10 +289,13 @@
     return high, low
 
 
-def rows_kernel(raw_ref, inverse_ref, out_ref, high_ref, low_ref):
+def rows_kernel(raw_ref, inverse_ref, out_ref, parts_ref):
     solved = dot_nt(raw_ref[...], inverse_ref[...])
     out_ref[...] = solved
-    high_ref[...], low_ref[...] = split(solved)
+    high, low = split(solved)
+    parts_ref[:, :TOTAL] = high
+    parts_ref[:, TOTAL : 2 * TOTAL] = high
+    parts_ref[:, 2 * TOTAL :] = low
 
 
 def solve_rows(raw, inverse):
@@ -272,19 +307,21 @@
         grid=(length // step,),
         out_shape=[
             jax.ShapeDtypeStruct((length, TOTAL), jnp.float32),
-            jax.ShapeDtypeStruct((length, TOTAL), jnp.bfloat16),
-            jax.ShapeDtypeStruct((length, TOTAL), jnp.bfloat16),
+            jax.ShapeDtypeStruct((length, 3 * TOTAL), jnp.bfloat16),
         ],
         in_specs=[block, pl.BlockSpec((TOTAL, TOTAL), lambda i: (0, 0))],
-        out_specs=[block, block, block],
+        out_specs=[block, pl.BlockSpec((step, 3 * TOTAL), lambda i: (i, 0))],
         compiler_params=pltpu.CompilerParams(vmem_limit_bytes=24 * MIB),
     )(raw, inverse)
 
 
-def cols_kernel(raw_ref, inverse_ref, out_ref, high_ref, low_ref):
+def cols_kernel(raw_ref, inverse_ref, out_ref, parts_ref):
     solved = dot_nt(inverse_ref[...], raw_ref[...])
     out_ref[...] = solved
-    high_ref[...], low_ref[...] = split(solved)
+    high, low = split(solved)
+    parts_ref[:TOTAL] = high
+    parts_ref[TOTAL : 2 * TOTAL] = low
+    parts_ref[2 * TOTAL :] = high
 
 
 def solve_cols(raw, inverse):
@@ -296,21 +333,20 @@
         grid=(length // step,),
         out_shape=[
             jax.ShapeDtypeStruct((TOTAL, length), jnp.float32),
-            jax.ShapeDtypeStruct((TOTAL, length), jnp.bfloat16),
-            jax.ShapeDtypeStruct((TOTAL, length), jnp.bfloat16),
+            jax.ShapeDtypeStruct((3 * TOTAL, length), jnp.bfloat16),
         ],
         in_specs=[
             pl.BlockSpec((step, TOTAL), lambda i: (i, 0)),
             pl.BlockSpec((TOTAL, TOTAL), lambda i: (0, 0)),
         ],
-        out_specs=[block, block, block],
+        out_specs=[block, pl.BlockSpec((3 * TOTAL, step), lambda i: (0, i))],
         compiler_params=pltpu.CompilerParams(vmem_limit_bytes=24 * MIB),
     )(raw, inverse)
 
 
 def final_kernel(
-    cols_blocks, code_ref, place_ref, front_ref, rows_ref, rows_high, rows_low, cols_ref, cols_high,
-    cols_low, lower_ref, arrived_ref, out_ref, cursor
+    cols_blocks, runs, code_ref, place_ref, front_ref, rows_ref, rows_parts, cols_ref, cols_parts,
+    lower_ref, arrived_ref, out_ref, cursor
 ):
     step = pl.program_id(0)
     sources, capacity = code_ref.shape
@@ -326,9 +362,7 @@
     chunk = min(512, width)
     for start in range(0, width, chunk):
         at = slice(start, start + chunk)
-        change = jnp.dot(rows_high[...], cols_high[:, at], preferred_element_type=jnp.float32)
-        change += jnp.dot(rows_high[...], cols_low[:, at], preferred_element_type=jnp.float32)
-        change += jnp.dot(rows_low[...], cols_high[:, at], preferred_element_type=jnp.float32)
+        change = jnp.dot(rows_parts[...], cols_parts[:, at], preferred_element_type=jnp.float32)
         out_ref[:, at] = front_ref[:, at] - change
 
     edge = (step + 1) * per_step * cols_blocks
@@ -343,10 +377,21 @@
             code = code_ref[s, k]
             unit_row = code // cols_blocks - step * per_step
             block_col = code % cols_blocks
-            rows = pl.ds(pl.multiple_of(unit_row * unit, unit), unit)
             columns = pl.ds(pl.multiple_of(block_col * side, side), side)
-            out_ref[rows, columns] += arrived_ref[s, k]
-            return k + 1
+            taken = jnp.int32(0)
+            for run in runs:
+                ending = code_ref[s, jnp.minimum(k + run - 1, capacity - 1)]
+                whole = (k + run <= capacity) & (ending == code + (run - 1) * cols_blocks)
+                use = whole & (ending < edge) & (taken == 0)
+
+                @pl.when(use)
+                def _():
+                    rows = pl.ds(pl.multiple_of(unit_row * unit, unit), run * unit)
+                    block = arrived_ref[s, pl.ds(k, run)]
+                    out_ref[rows, columns] += block.reshape(run * unit, side)
+
+                taken = jnp.where(use, run, taken)
+            return k + taken
 
         cursor[s] = lax.while_loop(more, add, cursor[s])
 
@@ -366,14 +411,17 @@
     height = TOTAL
     smem = pl.BlockSpec(memory_space=pltpu.SMEM)
     block = pl.BlockSpec((height, TOTAL), lambda i: (i, 0))
+    parts = pl.BlockSpec((height, 3 * TOTAL), lambda i: (i, 0))
     wide = pl.BlockSpec((height, col_len), lambda i: (i, 0))
     whole = pl.BlockSpec((TOTAL, col_len), lambda i: (0, 0))
-    return pl.pallas_call(
-        functools.partial(final_kernel, cols_blocks),
+    whole_parts = pl.BlockSpec((3 * TOTAL, col_len), lambda i: (0, 0))
+    runs = (8, 4, 1) if arrived.shape[2] == UNIT else (1,)
+    return pl.pallas_call(
+        functools.partial(final_kernel, cols_blocks, runs),
         grid=(row_len // height,),
         out_shape=jax.ShapeDtypeStruct((row_len, col_len), jnp.float32),
         in_specs=[
-            smem, smem, wide, block, block, block, whole, whole, whole,
+            smem, smem, wide, block, parts, whole, whole_parts,
             pl.BlockSpec((TOTAL, TOTAL), lambda i: (0, 0)),
             pl.BlockSpec(memory_space=pltpu.VMEM),
         ],
@@ -431,24 +479,39 @@
         (panel_key[:, :, None] == panel_key[:, None, :]) & (position[:, None, :] < position[:, :, None]),
         axis=2,
     )
-    ahead = (own(target_row) - row_now) % row_count
-    panel_slot = jnp.where(own(in_panel), ahead * capacity + own(panel_rank), -1)
-    panel_out = pack(tiles, panel_slot, valid_rows, row_count * capacity)
-    panel_in = [panel_out[:capacity]]
-    for shift in range(1, row_count):
-        sending = panel_out[shift * capacity : (shift + 1) * capacity]
-        turn = [(r, (r + shift) % row_count) for r in range(row_count)]
-        panel_in.append(lax.ppermute(sending, "row", turn))
     same_col = lax.dynamic_index_in_dim(
         jnp.stack([panel_key, panel_rank, code]).reshape(3, row_count, col_count, per_device),
         col_now, 2, keepdims=False,
     )
-    slots = jnp.arange(capacity)
-    fits = (same_col[0] == row_now)[:, :, None] & (same_col[1][:, :, None] == slots)
-    panel_code = same_col[2] // cols_blocks * PANELS + same_col[2] % cols_blocks
-    panel_codes = jnp.sum(jnp.where(fits, panel_code[:, :, None] + 1, 0), axis=1) - 1
-    by_shift = (row_now - jnp.arange(row_count)) % row_count
-    panel_codes = jnp.take(panel_codes, by_shift, axis=0).reshape(-1)
+
+    def send_panel(tiles, valid_rows, depth):
+        ahead = (own(target_row) - row_now) % row_count
+        fits = own(in_panel) & (own(panel_rank) < depth)
+        panel_slot = jnp.where(fits, ahead * depth + own(panel_rank), -1)
+        panel_out = pack(tiles, panel_slot, valid_rows, row_count * depth)
+        panel_in = [panel_out[:depth]]
+        for shift in range(1, row_count):
+            sending = panel_out[shift * depth : (shift + 1) * depth]
+            turn = [(r, (r + shift) % row_count) for r in range(row_count)]
+            panel_in.append(lax.ppermute(sending, "row", turn))
+        return panel_in
+
+    def sum_panel(front, panel_in, depth):
+        fits = (same_col[0] == row_now)[:, :, None] & (same_col[1][:, :, None] == jnp.arange(depth))
+        panel_code = same_col[2] // cols_blocks * PANELS + same_col[2] % cols_blocks
+        panel_codes = jnp.sum(jnp.where(fits, panel_code[:, :, None] + 1, 0), axis=1) - 1
+        by_shift = (row_now - jnp.arange(row_count)) % row_count
+        panel_codes = jnp.take(panel_codes, by_shift, axis=0).reshape(-1)
+        first = (col_now == 0).astype(jnp.int32).reshape(1)
+        partial = raw_panel(front, jnp.concatenate(panel_in, 0), panel_codes, first)
+        corner = jnp.where(row_now == 0, partial[:TOTAL], 0.0)
+        diagonal = corner
+        for other in range(1, row_count):
+            diagonal += lax.ppermute(corner, "row", [(0, other)])
+        return lax.psum((partial, diagonal), "col")
+
+    panel_depth = (capacity * 5 + 7) // 8
+    panel_in = send_panel(tiles, valid_rows, panel_depth)
 
     units = side // UNIT
     length = capacity * units
@@ -481,7 +544,7 @@
     empties = jnp.sum(jnp.where(listed, device_ids[:, :, None], 0), axis=1)
     free = jnp.sum(empty, axis=1)
     left = jnp.sum(jnp.maximum(load - width, 0), axis=1)
-    failed = jnp.any(left > free * width)
+    failed = jnp.any(left > free * width) | jnp.any(own(in_panel) & (own(panel_rank) >= panel_depth))
     counts = jnp.concatenate([jnp.sum(own_target < half_count)[None], free]).astype(jnp.int32)
     outgoing, sent_codes = spread(
         tiles, meta.astype(jnp.int32), empties.astype(jnp.int32), counts,
@@ -518,24 +581,33 @@
     relay_codes = lax.dynamic_slice_in_dim(notes, half_base, half_count, 0)[:, :pass_on]
     relay_slot = relay_slot.reshape(device_count, width)
 
-    first = (col_now == 0).astype(jnp.int32).reshape(1)
-    partial = raw_panel(front, jnp.concatenate(panel_in, 0), panel_codes, first)
-    raw_rows = lax.psum(partial, "col")
+    flat = relay_codes.reshape(-1)
+    unit_row, relay_col = flat // cols_blocks, flat % cols_blocks
+    wanted = (flat >= 0) & ((row_now > 0) | (unit_row >= TOTAL // UNIT))
+    wanted &= (col_now > 0) | (relay_col >= PANELS)
+    relay_block = unit_row // units * cols_blocks + relay_col
+    relay_key = jnp.where(wanted, relay_block * units + unit_row % units, local_codes)
+    relay_key = relay_key * flat.shape[0] + jnp.arange(flat.shape[0])
+    relay_order = jnp.sum(relay_key[None, :] < relay_key[:, None], axis=1)
+    listing = jnp.stack([relay_block, unit_row % units, jnp.arange(flat.shape[0])])
+    at_order = relay_order[None, :, None] == jnp.arange(flat.shape[0])
+    listing = jnp.sum(jnp.where(at_order, listing[:, :, None], 0), axis=1).astype(jnp.int32)
+    listing = [*listing, jnp.sum(wanted).astype(jnp.int32).reshape(1)]
+
+    raw_rows, diagonal = sum_panel(front, panel_in, panel_depth)
     slice_start = col_now * col_len % row_len
     slice_root = col_now * col_len // row_len
 
-    def chain(raw_rows):
+    def chain(raw_rows, diagonal):
         picked = lax.dynamic_slice_in_dim(raw_rows, slice_start, col_len, 0)
         raw_cols = lax.psum(jnp.where(row_now == slice_root, picked, 0.0), "row")
-        diagonal = jnp.where(row_now == 0, raw_rows[:TOTAL], jnp.eye(TOTAL, dtype=jnp.float32))
         lower, inverse = factor(diagonal)
-        inverse, raw_cols = lax.optimization_barrier((inverse, raw_cols))
-        inverse = lax.psum(jnp.where(row_now == 0, inverse, 0.0), "row")
         return solve_rows(raw_rows, inverse), solve_cols(raw_cols, inverse), lower
 
-    def relayed(front, tiles, valid_rows, outgoing, raw_rows):
+    def relayed(front, tiles, valid_rows, outgoing, raw_rows, diagonal):
         arrived = lax.all_to_all(outgoing, ("row", "col"), 0, 0, tiled=True)
-        rows, cols, lower = chain(raw_rows)
+        rows, cols, lower = chain(raw_rows, diagonal)
+        arrived, rows, cols, lower = lax.optimization_barrier((arrived, rows, cols, lower))
         passed = relay(relay_slot, arrived, half_count * pass_on)
         halves = [list(range(half_count)), list(range(half_count, device_count))]
         passed = lax.all_to_all(
@@ -543,24 +615,27 @@
             axis_index_groups=halves, tiled=True,
         )
         partial = finish(front, rows, cols, lower, arrived, direct_codes, place, cols_blocks)
-        return add_relayed(partial, passed, relay_codes, place, cols_blocks)
-
-    def padded(front, tiles, valid_rows, outgoing, raw_rows):
+        return add_relayed(partial, passed.reshape(-1, UNIT, side), listing, cols_blocks)
+
+    def padded(front, tiles, valid_rows, outgoing, raw_rows, diagonal):
+        raw_rows, diagonal = sum_panel(front, send_panel(tiles, valid_rows, capacity), capacity)
         order = (target * rows_blocks * cols_blocks + code) * per_device + position
         ranking = jnp.sum(
             (target[:, :, None] == target[:, None, :]) & (order[:, None, :] < order[:, :, None]), axis=2
         )
         slot = own(target) * capacity + own(ranking)
-        here = (target == device_now)[:, :, None] & (ranking[:, :, None] == slots)
+        here = (target == device_now)[:, :, None] & (ranking[:, :, None] == jnp.arange(capacity))
         codes = jnp.sum(jnp.where(here, code[:, :, None] + 1, 0), axis=1) - 1
         packed = pack(tiles, slot, valid_rows, device_count * capacity)
         arrived = lax.all_to_all(
             packed.reshape(device_count, capacity, side, side), ("row", "col"), 0, 0, tiled=True
         )
-        rows, cols, lower = chain(raw_rows)
+        rows, cols, lower = chain(raw_rows, diagonal)
         return finish(front, rows, cols, lower, arrived, codes, place, cols_blocks)
 
-    return lax.cond(too_full, padded, relayed, front, tiles, valid_rows, outgoing, raw_rows)
+    return lax.cond(
+        too_full, padded, relayed, front, tiles, valid_rows, outgoing, raw_rows, diagonal
+    )
 
 
 def solution(mesh):

time: 727 us -> 610 us (0.84)
  the two profiles are of different devices: /device:TPU:15 before, /device:TPU:18 now
where the time goes in v5:
time: 610 us; the launch traced here: 600 us
  waiting for transfers between devices  312 us (51%)
  Pallas kernels  126 us (21%)
  other arithmetic  75 us (12%)
  starting transfers between devices  37.3 us (6%)
  local copies, waits for them, and re-layouts  21.6 us (4%)
  between operations  16.8 us (3%)
  loops' own time  10.1 us (2%)
    psum x1, waiting for transfers between devices, chain(): raw_cols = lax.psum(jnp.where(row_now == slice_root, picked, 0.0), 'row')  129 us
    all_to_all x1, waiting for transfers between devices, relayed(): arrived = lax.all_to_all(outgoing, ('row', 'col'), 0, 0, tiled=True)  104 us
    psum x1, waiting for transfers between devices, sum_panel(): return lax.psum((partial, diagonal), 'col')  67.2 us
    pallas_call x1, Pallas kernels, finish(): pl.pallas_call(functools.partial(final_kernel, cols_blocks, runs), grid=(...  62.6 us
    another operation x6, other arithmetic, lower_of(): return jnp.linalg.cholesky(jnp.tril(block) + jnp.tril(block, -1).T)  24.8 us
    pallas_call x1, Pallas kernels, spread(): pl.pallas_call(functools.partial(spread_kernel, width, stride), out_shape...  23.6 us
    another operation x4, other arithmetic, inverse_of(): jax.scipy.linalg.solve_triangular(block, jnp.eye(NB, dtype=jnp.float32),...  21.1 us
    all_to_all x1, starting transfers between devices, body(): lax.all_to_all(notes.reshape(device_count, pass_on + 1), ('row', 'col'),...  14.5 us
  transfers between devices with their start and end apart: 12, of which 5 were waited for; matrix products, arithmetic and copies ran while one was open for 13% of the time, Pallas kernels for 16%

profile of v5, /device:TPU:18, one launch (start us, length us, event | category | flops | bytes accessed | tf_op | source)
XLA Modules:
  0.0 600.3 jit_solution(11796677186166574363)
XLA Ops:
  9.4 7.7 %shard_map.49 = f32[20,128,128]{2,1,0:T(8,128)S(1)} custom-call(s32[128]{0:T(128)S(1)} %get-tuple-element.361.slot_ref, s32[128]{0:T(128)} %valid_ref.1, f32[128,128,128]{2,1,0:T(8,128)} %tiles_ref.1), custom_call_target="tpu_custom_call" | custom-call | tf_op jit(solution)/shard_map/pallas_call | solution.py:53
  17.6 3.7 collective-permute-start.7
  23.2 23.6 %shard_map.48 = (f32[32,84,8,128]{3,2,1,0:T(8,128)}, s32[32,128]{1,0:T(8,128)}) custom-call(s32[6,128]{1,0:T(8,128)S(1)} %select_reduce_fusion.8.meta_ref, s32[2,16]{1,0:T(2,128)S(1)} %select_reduce_fusion.10.empty_ref, s32[3]{0:T(128)S(1)} %pad_add_fusion.1.count_ref, f32[128,16,8,128]{3,2,1,0:T(8,128)} %bitcast.158), custom_call_target="tpu_custom_call" | custom-call | tf_op jit(solution)/shard_map/pallas_call | solution.py:118
  46.8 5.4 all-to-all-start.3
  58.1 5.8 convert_reduce_fusion.1
  64.2 3.0 shard_map.50
  67.2 2.0 copy-done.1
  73.2 7.9 %collective-permute-done.10 = f32[256,256]{1,0:T(8,128)S(1)} collective-permute-done((f32[256,256]{1,0:T(8,128)S(1)}, f32[256,256]{1,0:T(8,128)S(1)}, u32[]{:S(2)}, u32[]{:S(2)}) %collective-permute-start.10) | collective-permute-done | bytes 262176 | tf_op jit(solution)/shard_map/ppermute | solution.py:510
  81.2 1.7 add_add_fusion.1
  87.9 14.5 %all-to-all-start.4 = ((s32[32,1,49]{2,1,0:T(1,128)}), s32[32,1,49]{2,1,0:T(1,128)S(1)}, u32[]{:S(2)}, u32[]{:S(2)}) async-start(s32[32,1,49]{2,1,0:T(1,128)} %bitcast.51), calls=%async_computation.4 | async-start | bytes 32768 | tf_op jit(solution)/shard_map/all_to_all | solution.py:577
  102.3 4.1 all-to-all-done.4
  108.1 1.7 compare_convert_fusion
  109.8 67.2 %all-reduce.17.cloned.1.call-done = (f32[256,256]{1,0:T(8,128)}, f32[4096,256]{1,0:T(8,128)}) async-done(((f32[256,256]{1,0:T(8,128)}, f32[4096,256]{1,0:T(8,128)}), (f32[256,256]{1,0:T(8,128)}, f32[4096,256]{1,0:T(8,128)})) %all-reduce.17.cloned.1.call-update) | async-done | bytes 4456464 | tf_op jit(solution)/shard_map/psum | solution.py:511
  178.6 414.3 %conditional.1 = (f32[4096,2048]{1,0:T(8,128)}) conditional(s32[]{:T(128)} %convert_element_type.57, (s32[768,768]{1,0:T(8,128)}, s32[768,768]{1,0:T(8,128)}, s32[3,768]{1,0:T(4,128)S(1)}, s32[16,48]{1,0:T(8,128)S(1)}, s32[32,84]{1,0:T(8,128)S(1)}, /*index=5*/s32[32,84]{1,0:T(8,128)S(1)}, pred[32,84]{1,0:T(8,128)(4,1)S(1)}, ...), branch_computations={%region_19.28_spmd, %region_26.35_spmd} | conditional | flops 158961056 | bytes 291201664 | solution.py:636
  178.6 5.0 all-to-all-start
  183.8 3.1 dynamic-slice_select_fusion.1
  187.4 11.7 %cholesky.74 = f32[128,128]{1,0:T(8,128)S(1)} custom-call(f32[128,128]{1,0:T(8,128)S(1)} %copy.123), custom_call_target="Cholesky" | custom-call | tf_op jit(solution)/shard_map/cond/branch_0_fun/jit(cholesky)/cholesky | solution.py:436
  200.5 9.8 %custom-call.8 = f32[1,128,128]{1,2,0:T(8,128)S(1)} custom-call(f32[1,128,128]{2,1,0:T(8,128)S(1)} %get-tuple-element.324), custom_call_target="InvertDiagBlocksLowerTriangular" | custom-call | tf_op jit(solution)/shard_map/cond/branch_0_fun/jit(_solve_triangular)/triangular_solve | solution.py:439
  211.7 11.7 %cholesky.85 = f32[128,128]{1,0:T(8,128)S(1)} custom-call(f32[128,128]{1,0:T(8,128)S(1)} %fusion.37), custom_call_target="Cholesky" | custom-call | tf_op jit(solution)/shard_map/cond/branch_0_fun/jit(cholesky)/cholesky | solution.py:436
  224.8 10.0 %custom-call.9 = f32[1,128,128]{1,2,0:T(8,128)S(1)} custom-call(f32[1,128,128]{2,1,0:T(8,128)S(1)} %get-tuple-element.322), custom_call_target="InvertDiagBlocksLowerTriangular" | custom-call | tf_op jit(solution)/shard_map/cond/branch_0_fun/jit(_solve_triangular)/triangular_solve | solution.py:439
  235.8 7.5 %branch_0_fun.5 = (f32[4096,256]{1,0:T(8,128)S(1)}, bf16[4096,768]{1,0:T(8,128)(2,1)S(1)}) custom-call(f32[4096,256]{1,0:T(8,128)} %get-tuple-element.191.raw_ref, f32[256,256]{1,0:T(8,128)S(1)} %select_maximum_fusion.3.inverse_ref), custom_call_target="tpu_custom_call" | custom-call | tf_op jit(solution)/shard_map/cond/branch_0_fun/pallas_call | solution.py:305
  243.2 2.6 copy-done.5
  245.8 2.0 copy-done.7
  248.6 128.6 %all-reduce.11.cloned.1.call-done.raw_ref = f32[2048,256]{1,0:T(8,128)} async-done(((f32[2048,256]{1,0:T(8,128)}), f32[2048,256]{1,0:T(8,128)}) %all-reduce.11.cloned.1.call-update) | async-done | bytes 2097168 | tf_op jit(solution)/shard_map/cond/branch_0_fun/psum | solution.py:603
  378.8 3.0 branch_0_fun.6
  384.8 104.3 %all-to-all-done.arrived_ref = f32[32,84,8,128]{3,2,1,0:T(8,128)} async-done(((f32[32,84,8,128]{3,2,1,0:T(8,128)}), f32[32,84,8,128]{3,2,1,0:T(8,128)}, u32[]{:S(2)}, u32[]{:S(2)}) %all-to-all-start) | async-done | bytes 11010080 | tf_op jit(solution)/shard_map/cond/branch_0_fun/all_to_all | solution.py:608
  489.1 8.2 %branch_0_fun.8 = f32[768,8,128]{2,1,0:T(8,128)S(1)} custom-call(s32[32,84]{1,0:T(8,128)S(1)} %get-tuple-element.320.slot_ref, f32[32,84,8,128]{3,2,1,0:T(8,128)} %all-to-all-done.arrived_ref), custom_call_target="tpu_custom_call" | custom-call | tf_op jit(solution)/shard_map/cond/branch_0_fun/pallas_call | solution.py:151
  498.9 5.5 all-to-all-start.1
  505.1 1.8 reduce_sum.148
  506.9 2.1 broadcast_compare_fusion.1
  510.5 62.6 %branch_0_fun.7.partial_ref = f32[4096,2048]{1,0:T(8,128)} custom-call(s32[32,84]{1,0:T(8,128)} %fusion.45.code_ref, s32[2]{0:T(128)S(1)} %copy-done.21, f32[4096,2048]{1,0:T(8,128)} %get-tuple-element.189.front_ref, f32[4096,256]{1,0:T(8,128)} %copy-done.7, bf16[4096,768]{1,0:T(8,128)(2,1)} %copy-done.5, f32[256,2048]{1,0:T(8,128)} %copy-done.11, ...), custom_call_target="tpu_custom_call" | custom-call | tf_op jit(solution)/shard_map/cond/branch_0_fun/pallas_call | solution.py:419
  573.1 10.0 %branch_0_fun.9 = f32[4096,2048]{1,0:T(8,128)} custom-call(s32[768]{0:T(1024)S(1)} %get-tuple-element.309.block_ref, s32[768]{0:T(1024)S(1)} %get-tuple-element.308.unit_ref, s32[768]{0:T(1024)S(1)} %get-tuple-element.307.index_ref, s32[1]{0:T(128)} %bitcast.count_ref, f32[4096,2048]{1,0:T(8,128)} %branch_0_fun.7.partial_ref, ...), custom_call_target="tpu_custom_call", output_to_operand_aliasing={{}: (4, {})} | custom-call | tf_op jit(solution)/shard_map/cond/branch_0_fun/pallas_call | solution.py:230
  (149 shorter events, 35.4 us)
Async XLA Ops:
  7.4 9.7 %copy-start.17 = (s32[32,128]{1,0:T(8,128)}, s32[32,128]{1,0:T(8,128)S(1)}, u32[]{:S(2)}) copy-start(s32[32,128]{1,0:T(8,128)S(1)} %get-tuple-element.354) | copy-start | bytes 49156
  7.5 47.5 %copy-start.20 = (pred[32,128]{1,0:T(8,128)(4,1)}, pred[32,128]{1,0:T(8,128)(4,1)S(1)}, u32[]{:S(2)}) copy-start(pred[32,128]{1,0:T(8,128)(4,1)S(1)} %get-tuple-element.329) | copy-start | bytes 12292
  17.2 4.1 copy-start.18
  17.3 46.8 %collective-permute-start.8 = (f32[5,128,128]{2,1,0:T(8,128)S(1)}, f32[5,128,128]{2,1,0:T(8,128)S(1)}, u32[]{:S(2)}, u32[]{:S(2)}) collective-permute-start(f32[5,128,128]{2,1,0:T(8,128)S(1)} %get-tuple-element.343), channel_id=1, source_target_pairs={{0,24},{8,0},{16,8},{24,16},{1,25},{9,1},{17,9},{25,17},{2,26},{10... | collective-permute-start | bytes 983048 | tf_op jit(solution)/shard_map/ppermute | solution.py:496
  17.6 46.5 %collective-permute-start.7 = (f32[5,128,128]{2,1,0:T(8,128)S(1)}, f32[5,128,128]{2,1,0:T(8,128)S(1)}, u32[]{:S(2)}, u32[]{:S(2)}) collective-permute-start(f32[5,128,128]{2,1,0:T(8,128)S(1)} %get-tuple-element.344), channel_id=1, source_target_pairs={{0,16},{8,24},{16,0},{24,8},{1,17},{9,25},{17,1},{25,9},{2,18},{10... | collective-permute-start | bytes 983048 | tf_op jit(solution)/shard_map/ppermute | solution.py:496
  21.3 42.8 %collective-permute-start.6 = (f32[5,128,128]{2,1,0:T(8,128)S(1)}, f32[5,128,128]{2,1,0:T(8,128)S(1)}, u32[]{:S(2)}, u32[]{:S(2)}) collective-permute-start(f32[5,128,128]{2,1,0:T(8,128)S(1)} %get-tuple-element.345), channel_id=1, source_target_pairs={{0,8},{8,16},{16,24},{24,0},{1,9},{9,17},{17,25},{25,1},{2,10},{10... | collective-permute-start | bytes 983048 | tf_op jit(solution)/shard_map/ppermute | solution.py:496
  46.8 9.9 %all-to-all-start.3 = ((s32[32,1,84]{2,1,0:T(1,128)}), s32[32,1,84]{2,1,0:T(1,128)S(1)}, u32[]{:S(2)}, u32[]{:S(2)}) async-start(s32[32,1,84]{2,1,0:T(1,128)} %bitcast.43), calls=%async_computation.3 | async-start | bytes 32768 | tf_op jit(solution)/shard_map/all_to_all | solution.py:554
  52.3 124.7 %all-reduce.17.cloned.1.call-start = ((), (), s32[]{:S(2)}) async-start(), calls=%async_computation.8 | async-start | bytes 8912896 | tf_op jit(solution)/shard_map/psum | solution.py:511
  67.2 2.0 copy-start.1
  69.2 11.9 %collective-permute-start.10 = (f32[256,256]{1,0:T(8,128)S(1)}, f32[256,256]{1,0:T(8,128)S(1)}, u32[]{:S(2)}, u32[]{:S(2)}) collective-permute-start(f32[256,256]{1,0:T(8,128)S(1)} %slice_select_fusion.1), channel_id=1, source_target_pairs={{0,16},{1,17},{2,18},{3,19},{4,20},{5,21},{6,22},{7,23}} | collective-permute-start | bytes 786440 | tf_op jit(solution)/shard_map/ppermute | solution.py:510
  70.5 10.6 %collective-permute-start.11 = (f32[256,256]{1,0:T(8,128)S(1)}, f32[256,256]{1,0:T(8,128)S(1)}, u32[]{:S(2)}, u32[]{:S(2)}) collective-permute-start(f32[256,256]{1,0:T(8,128)S(1)} %slice_select_fusion.1), channel_id=1, source_target_pairs={{0,24},{1,25},{2,26},{3,27},{4,28},{5,29},{6,30},{7,31}} | collective-permute-start | bytes 786440 | tf_op jit(solution)/shard_map/ppermute | solution.py:510
  71.2 10.0 %collective-permute-start.9 = (f32[256,256]{1,0:T(8,128)S(1)}, f32[256,256]{1,0:T(8,128)S(1)}, u32[]{:S(2)}, u32[]{:S(2)}) collective-permute-start(f32[256,256]{1,0:T(8,128)S(1)} %slice_select_fusion.1), channel_id=1, source_target_pairs={{0,8},{1,9},{2,10},{3,11},{4,12},{5,13},{6,14},{7,15}} | collective-permute-start | bytes 786440 | tf_op jit(solution)/shard_map/ppermute | solution.py:510
  87.9 18.6 %all-to-all-start.4 = ((s32[32,1,49]{2,1,0:T(1,128)}), s32[32,1,49]{2,1,0:T(1,128)S(1)}, u32[]{:S(2)}, u32[]{:S(2)}) async-start(s32[32,1,49]{2,1,0:T(1,128)} %bitcast.51), calls=%async_computation.4 | async-start | bytes 32768 | tf_op jit(solution)/shard_map/all_to_all | solution.py:577
  177.0 1.6 copy-start.15
  178.6 310.5 %all-to-all-start = ((f32[32,84,8,128]{3,2,1,0:T(8,128)}), f32[32,84,8,128]{3,2,1,0:T(8,128)}, u32[]{:S(2)}, u32[]{:S(2)}) async-start(f32[32,84,8,128]{3,2,1,0:T(8,128)} %get-tuple-element.190), calls=%async_computation | async-start | bytes 22020096 | tf_op jit(solution)/shard_map/cond/branch_0_fun/all_to_all | solution.py:608
  183.5 193.7 %all-reduce.11.cloned.1.call-start = ((), (), s32[]{:S(2)}) async-start(), calls=%async_computation.5 | async-start | bytes 4194304 | tf_op jit(solution)/shard_map/cond/branch_0_fun/psum | solution.py:603
  243.2 2.6 copy-start.5
  245.8 2.0 copy-start.7
  377.2 1.6 copy-start.13
  381.8 1.7 copy-start.9
  383.5 1.3 copy-start.11
  497.3 1.6 copy-start.3
  498.9 74.2 %all-to-all-start.1 = ((f32[16,48,8,128]{3,2,1,0:T(8,128)}), f32[16,48,8,128]{3,2,1,0:T(8,128)S(1)}, u32[]{:S(2)}, u32[]{:S(2)}) async-start(f32[16,48,8,128]{3,2,1,0:T(8,128)} %bitcast.157), calls=%async_computation.1 | async-start | bytes 6291456 | tf_op jit(solution)/shard_map/cond/branch_0_fun/all_to_all | solution.py:613
  506.9 3.5 copy-start.21
Sparse Core Ops, SparseCore 0:
  83.0 93.9 all-reduce.16
  187.0 190.1 all-reduce.10

commit v6 on v5

--- a/solution.py
+++ b/solution.py
@@ -345,7 +345,7 @@
 
 
 def final_kernel(
-    cols_blocks, runs, code_ref, place_ref, front_ref, rows_ref, rows_parts, cols_ref, cols_parts,
+    cols_blocks, runs, code_ref, run_ref, place_ref, front_ref, rows_ref, rows_parts, cols_ref, cols_parts,
     lower_ref, arrived_ref, out_ref, cursor
 ):
     step = pl.program_id(0)
@@ -375,23 +375,19 @@
 
         def add(k):
             code = code_ref[s, k]
+            length = run_ref[s, k]
             unit_row = code // cols_blocks - step * per_step
-            block_col = code % cols_blocks
-            columns = pl.ds(pl.multiple_of(block_col * side, side), side)
-            taken = jnp.int32(0)
+            columns = pl.ds(pl.multiple_of(code % cols_blocks * side, side), side)
             for run in runs:
-                ending = code_ref[s, jnp.minimum(k + run - 1, capacity - 1)]
-                whole = (k + run <= capacity) & (ending == code + (run - 1) * cols_blocks)
-                use = whole & (ending < edge) & (taken == 0)
-
-                @pl.when(use)
+                skipped = length // (2 * run) * (2 * run)
+
+                @pl.when(length // run % 2 == 1)
                 def _():
-                    rows = pl.ds(pl.multiple_of(unit_row * unit, unit), run * unit)
-                    block = arrived_ref[s, pl.ds(k, run)]
+                    rows = pl.ds(pl.multiple_of((unit_row + skipped) * unit, unit), run * unit)
+                    block = arrived_ref[s, pl.ds(k + skipped, run)]
                     out_ref[rows, columns] += block.reshape(run * unit, side)
 
-                taken = jnp.where(use, run, taken)
-            return k + taken
+            return k + length
 
         cursor[s] = lax.while_loop(more, add, cursor[s])
 
@@ -406,7 +402,7 @@
         out_ref[:, :TOTAL] = jnp.where(top, lower_ref[...], rows_ref[...])
 
 
-def finish(front, rows, cols, lower, arrived, codes, place, cols_blocks):
+def finish(front, rows, cols, lower, arrived, codes, lengths, place, cols_blocks):
     row_len, col_len = front.shape
     height = TOTAL
     smem = pl.BlockSpec(memory_space=pltpu.SMEM)
@@ -415,20 +411,20 @@
     wide = pl.BlockSpec((height, col_len), lambda i: (i, 0))
     whole = pl.BlockSpec((TOTAL, col_len), lambda i: (0, 0))
     whole_parts = pl.BlockSpec((3 * TOTAL, col_len), lambda i: (0, 0))
-    runs = (8, 4, 1) if arrived.shape[2] == UNIT else (1,)
+    runs = (16, 8, 4, 2, 1) if arrived.shape[2] == UNIT else (1,)
     return pl.pallas_call(
         functools.partial(final_kernel, cols_blocks, runs),
         grid=(row_len // height,),
         out_shape=jax.ShapeDtypeStruct((row_len, col_len), jnp.float32),
         in_specs=[
-            smem, smem, wide, block, parts, whole, whole_parts,
+            smem, smem, smem, wide, block, parts, whole, whole_parts,
             pl.BlockSpec((TOTAL, TOTAL), lambda i: (0, 0)),
             pl.BlockSpec(memory_space=pltpu.VMEM),
         ],
         out_specs=wide,
         scratch_shapes=[pltpu.SMEM((codes.shape[0],), jnp.int32)],
         compiler_params=pltpu.CompilerParams(vmem_limit_bytes=56 * MIB),
-    )(codes, place, front, *rows, *cols, lower, arrived)
+    )(codes, lengths, place, front, *rows, *cols, lower, arrived)
 
 
 def factor(diagonal):
@@ -503,12 +499,14 @@
         by_shift = (row_now - jnp.arange(row_count)) % row_count
         panel_codes = jnp.take(panel_codes, by_shift, axis=0).reshape(-1)
         first = (col_now == 0).astype(jnp.int32).reshape(1)
-        partial = raw_panel(front, jnp.concatenate(panel_in, 0), panel_codes, first)
+        return raw_panel(front, jnp.concatenate(panel_in, 0), panel_codes, first)
+
+    def sum_corner(partial):
         corner = jnp.where(row_now == 0, partial[:TOTAL], 0.0)
         diagonal = corner
         for other in range(1, row_count):
             diagonal += lax.ppermute(corner, "row", [(0, other)])
-        return lax.psum((partial, diagonal), "col")
+        return diagonal
 
     panel_depth = (capacity * 5 + 7) // 8
     panel_in = send_panel(tiles, valid_rows, panel_depth)
@@ -551,11 +549,18 @@
         device_count, width, length, cols_blocks,
     )
 
+    partial = sum_panel(front, panel_in, panel_depth)
+    partial, sent_codes = lax.optimization_barrier((partial, sent_codes))
+    diagonal = sum_corner(partial)
     got = lax.all_to_all(sent_codes[:, :width], ("row", "col"), 0, 0, tiled=True)
     got_target = got // local_codes
     local = got % local_codes
     mine = (got >= 0) & (got_target == device_now)
     direct_codes = jnp.where(mine, local, -1)
+    steps = jnp.arange(width)
+    opening = (local // cols_blocks % units == 0) | jnp.logical_not(mine)
+    later = (steps[None, :] > steps[:, None]) & opening[:, None, :]
+    direct_runs = jnp.min(jnp.where(later, steps, width), axis=2) - steps
     total_units = device_count * width
     passing = ((got >= 0) & (got_target != device_now)).reshape(-1)
     flat_key = jnp.where(passing, got.reshape(-1) * total_units + jnp.arange(total_units), -1)
@@ -594,7 +599,9 @@
     listing = jnp.sum(jnp.where(at_order, listing[:, :, None], 0), axis=1).astype(jnp.int32)
     listing = [*listing, jnp.sum(wanted).astype(jnp.int32).reshape(1)]
 
-    raw_rows, diagonal = sum_panel(front, panel_in, panel_depth)
+    outgoing, notes, diagonal, partial = lax.optimization_barrier((outgoing, notes, diagonal, partial))
+    raw_rows, diagonal = lax.psum((partial, diagonal), "col")
+    arrived = lax.all_to_all(outgoing, ("row", "col"), 0, 0, tiled=True)
     slice_start = col_now * col_len % row_len
     slice_root = col_now * col_len // row_len
 
@@ -604,21 +611,24 @@
         lower, inverse = factor(diagonal)
         return solve_rows(raw_rows, inverse), solve_cols(raw_cols, inverse), lower
 
-    def relayed(front, tiles, valid_rows, outgoing, raw_rows, diagonal):
-        arrived = lax.all_to_all(outgoing, ("row", "col"), 0, 0, tiled=True)
-        rows, cols, lower = chain(raw_rows, diagonal)
-        arrived, rows, cols, lower = lax.optimization_barrier((arrived, rows, cols, lower))
+    rows, cols, lower = chain(raw_rows, diagonal)
+    arrived, rows, cols, lower = lax.optimization_barrier((arrived, rows, cols, lower))
+
+    def relayed(front, tiles, valid_rows, arrived, rows, cols, lower):
         passed = relay(relay_slot, arrived, half_count * pass_on)
         halves = [list(range(half_count)), list(range(half_count, device_count))]
         passed = lax.all_to_all(
             passed.reshape(half_count, pass_on, UNIT, side), ("row", "col"), 0, 0,
             axis_index_groups=halves, tiled=True,
         )
-        partial = finish(front, rows, cols, lower, arrived, direct_codes, place, cols_blocks)
+        partial = finish(
+            front, rows, cols, lower, arrived, direct_codes, direct_runs, place, cols_blocks
+        )
         return add_relayed(partial, passed.reshape(-1, UNIT, side), listing, cols_blocks)
 
-    def padded(front, tiles, valid_rows, outgoing, raw_rows, diagonal):
-        raw_rows, diagonal = sum_panel(front, send_panel(tiles, valid_rows, capacity), capacity)
+    def padded(front, tiles, valid_rows, arrived, rows, cols, lower):
+        partial = sum_panel(front, send_panel(tiles, valid_rows, capacity), capacity)
+        raw_rows, diagonal = lax.psum((partial, sum_corner(partial)), "col")
         order = (target * rows_blocks * cols_blocks + code) * per_device + position
         ranking = jnp.sum(
             (target[:, :, None] == target[:, None, :]) & (order[:, None, :] < order[:, :, None]), axis=2
@@ -631,10 +641,12 @@
             packed.reshape(device_count, capacity, side, side), ("row", "col"), 0, 0, tiled=True
         )
         rows, cols, lower = chain(raw_rows, diagonal)
-        return finish(front, rows, cols, lower, arrived, codes, place, cols_blocks)
+        return finish(
+            front, rows, cols, lower, arrived, codes, jnp.ones_like(codes), place, cols_blocks
+        )
 
     return lax.cond(
-        too_full, padded, relayed, front, tiles, valid_rows, outgoing, raw_rows, diagonal
+        too_full, padded, relayed, front, tiles, valid_rows, arrived, rows, cols, lower
     )
 
 

time: 610 us -> 544 us (0.89)
  the two profiles are of different devices: /device:TPU:18 before, /device:TPU:7 now
where the time goes in v6:
time: 544 us; the launch traced here: 535 us
  waiting for transfers between devices  262 us (48%)
  Pallas kernels  111 us (20%)
  other arithmetic  83.9 us (15%)
  starting transfers between devices  31.5 us (6%)
  local copies, waits for them, and re-layouts  26.7 us (5%)
  between operations  17.3 us (3%)
    psum x1, waiting for transfers between devices, body(): raw_rows, diagonal = lax.psum((partial, diagonal), 'col')  208 us
    psum x1, waiting for transfers between devices, chain(): raw_cols = lax.psum(jnp.where(row_now == slice_root, picked, 0.0), 'row')  51.6 us
    pallas_call x1, Pallas kernels, finish(): pl.pallas_call(functools.partial(final_kernel, cols_blocks, runs), grid=(...  49.3 us
    another operation x6, other arithmetic, lower_of(): return jnp.linalg.cholesky(jnp.tril(block) + jnp.tril(block, -1).T)  24.8 us
    another operation x4, other arithmetic, inverse_of(): jax.scipy.linalg.solve_triangular(block, jnp.eye(NB, dtype=jnp.float32),...  21 us
    pallas_call x1, Pallas kernels, spread(): pl.pallas_call(functools.partial(spread_kernel, width, stride), out_shape...  21 us
  transfers between devices with their start and end apart: 12, of which 3 were waited for; matrix products, arithmetic and copies ran while one was open for 17% of the time, Pallas kernels for 15%

profile of v6, /device:TPU:7, one launch (start us, length us, event | category | flops | bytes accessed | tf_op | source)
XLA Modules:
  0.0 535.2 jit_solution(5628290993252598221)
XLA Ops:
  9.4 7.7 %shard_map.48 = f32[20,128,128]{2,1,0:T(8,128)S(1)} custom-call(s32[128]{0:T(128)S(1)} %get-tuple-element.555.slot_ref, s32[128]{0:T(128)} %valid_ref.1, f32[128,128,128]{2,1,0:T(8,128)} %tiles_ref.1), custom_call_target="tpu_custom_call" | custom-call | tf_op jit(solution)/shard_map/pallas_call | solution.py:53
  17.2 3.4 collective-permute-start.8
  27.2 21.0 %shard_map.50 = (f32[32,84,8,128]{3,2,1,0:T(8,128)S(1)}, s32[32,128]{1,0:T(8,128)}) custom-call(s32[6,128]{1,0:T(8,128)S(1)} %select_reduce_fusion.7.meta_ref, s32[2,16]{1,0:T(2,128)S(1)} %select_reduce_fusion.11.empty_ref, s32[3]{0:T(128)S(1)} %pad_add_fusion.1.count_ref, f32[128,16,8,128]{3,2,1,0:T(8,128)} %bitcast.161), custom_call_target="tpu_custom_call" | custom-call | tf_op jit(solution)/shard_map/pallas_call | solution.py:118
  48.2 4.2 copy-done.4
  52.6 3.0 shard_map.49
  55.6 1.9 copy-done.1
  57.5 5.5 %all-to-all-start.2 = ((s32[32,1,84]{2,1,0:T(1,128)}), s32[32,1,84]{2,1,0:T(1,128)S(1)}, u32[]{:S(2)}, u32[]{:S(2)}) async-start(s32[32,1,84]{2,1,0:T(1,128)} %bitcast.46), calls=%async_computation.2 | async-start | bytes 32768 | tf_op jit(solution)/shard_map/all_to_all | solution.py:555
  63.9 4.0 collective-permute-start.10
  68.0 1.6 collective-permute-start.11
  72.4 5.8 %convert_reduce_fusion.1 = s32[2688]{0:T(1024)S(1)} fusion(s32[2688]{0:T(1024)S(1)} %get-tuple-element.550, s32[2688]{0:T(1024)S(1)} %get-tuple-element.549), kind=kLoop, calls=%fused_computation.128 | loop fusion | flops 36124032 | bytes 32256 | tf_op jit(solution)/shard_map/reduce_sum | solution.py:568
  85.4 3.3 all-to-all-start.3
  88.7 1.7 add_add_fusion.1
  90.4 3.0 all-to-all-done.3
  93.4 6.0 %all-to-all-start.4 = ((f32[32,84,8,128]{3,2,1,0:T(8,128)}), f32[32,84,8,128]{3,2,1,0:T(8,128)}, u32[]{:S(2)}, u32[]{:S(2)}) async-start(f32[32,84,8,128]{3,2,1,0:T(8,128)} %copy-done.4), calls=%async_computation.4 | async-start | bytes 22020096 | tf_op jit(solution)/shard_map/all_to_all | solution.py:604
  105.6 207.6 %all-reduce.17.cloned.1.call-done = (f32[4096,256]{1,0:T(8,128)}, f32[256,256]{1,0:T(8,128)}) async-done(((f32[4096,256]{1,0:T(8,128)}, f32[256,256]{1,0:T(8,128)}), (f32[4096,256]{1,0:T(8,128)}, f32[256,256]{1,0:T(8,128)})) %all-reduce.17.cloned.1.call-update) | async-done | bytes 4456464 | tf_op jit(solution)/shard_map/psum | solution.py:603
  315.2 11.7 %cholesky.96 = f32[128,128]{1,0:T(8,128)S(1)} custom-call(f32[128,128]{1,0:T(8,128)S(1)} %fusion.52), custom_call_target="Cholesky" | custom-call | tf_op jit(solution)/shard_map/jit(cholesky)/cholesky | solution.py:432
  328.3 9.8 %custom-call.10 = f32[1,128,128]{1,2,0:T(8,128)S(1)} custom-call(f32[1,128,128]{2,1,0:T(8,128)S(1)} %get-tuple-element.515), custom_call_target="InvertDiagBlocksLowerTriangular" | custom-call | tf_op jit(solution)/shard_map/jit(_solve_triangular)/triangular_solve | solution.py:435
  338.1 3.1 dynamic-slice_select_fusion.1
  342.5 11.7 %cholesky.107 = f32[128,128]{1,0:T(8,128)S(1)} custom-call(f32[128,128]{1,0:T(8,128)S(1)} %fusion.50), custom_call_target="Cholesky" | custom-call | tf_op jit(solution)/shard_map/jit(cholesky)/cholesky | solution.py:432
  355.5 10.0 %custom-call.11 = f32[1,128,128]{1,2,0:T(8,128)S(1)} custom-call(f32[1,128,128]{2,1,0:T(8,128)S(1)} %get-tuple-element.513), custom_call_target="InvertDiagBlocksLowerTriangular" | custom-call | tf_op jit(solution)/shard_map/jit(_solve_triangular)/triangular_solve | solution.py:435
  366.5 2.2 copy-done.5
  368.7 7.5 %shard_map.51 = (f32[4096,256]{1,0:T(8,128)}, bf16[4096,768]{1,0:T(8,128)(2,1)}) custom-call(f32[4096,256]{1,0:T(8,128)S(1)} %copy-done.5, f32[256,256]{1,0:T(8,128)S(1)} %select_maximum_fusion.3.inverse_ref), custom_call_target="tpu_custom_call" | custom-call | tf_op jit(solution)/shard_map/pallas_call | solution.py:305
  376.3 51.6 %all-reduce.15.cloned.1.call-done.raw_ref = f32[2048,256]{1,0:T(8,128)} async-done(((f32[2048,256]{1,0:T(8,128)}), f32[2048,256]{1,0:T(8,128)}) %all-reduce.15.cloned.1.call-update) | async-done | bytes 2097168 | tf_op jit(solution)/shard_map/psum | solution.py:610
  429.5 4.3 shard_map.52
  440.1 87.7 %conditional.1 = (f32[4096,2048]{1,0:T(8,128)}) conditional(s32[]{:T(128)} %convert_element_type.57, (s32[768,768]{1,0:T(8,128)}, s32[768,768]{1,0:T(8,128)}, s32[3,768]{1,0:T(4,128)S(1)}, s32[16,48]{1,0:T(8,128)}, s32[32,84]{1,0:T(8,128)S(1)}, /*index=5*/s32[32,84]{1,0:T(8,128)S(1)}, pred[32,84]{1,0:T(8,128)(4,1)S(1)}, ...), branch_computations={%region_22.29_spmd, %region_27.36_spmd} | conditional | flops 158961056 | bytes 291225216 | solution.py:648
  440.9 8.3 %branch_0_fun.4 = f32[768,8,128]{2,1,0:T(8,128)S(1)} custom-call(s32[32,84]{1,0:T(8,128)S(1)} %get-tuple-element.509.slot_ref, f32[32,84,8,128]{3,2,1,0:T(8,128)} %get-tuple-element.264.arrived_ref), custom_call_target="tpu_custom_call" | custom-call | tf_op jit(solution)/shard_map/cond/branch_0_fun/pallas_call | solution.py:151
  449.2 1.7 copy-done.3
  451.0 5.5 %all-to-all-start = ((f32[16,48,8,128]{3,2,1,0:T(8,128)}), f32[16,48,8,128]{3,2,1,0:T(8,128)S(1)}, u32[]{:S(2)}, u32[]{:S(2)}) async-start(f32[16,48,8,128]{3,2,1,0:T(8,128)} %bitcast.160), calls=%async_computation | async-start | bytes 6291456 | tf_op jit(solution)/shard_map/cond/branch_0_fun/all_to_all | solution.py:620
  457.8 2.4 reduce_sum.148
  461.9 2.0 select_reduce_fusion.5
  466.5 49.3 %branch_0_fun.3.partial_ref = f32[4096,2048]{1,0:T(8,128)} custom-call(s32[32,84]{1,0:T(8,128)} %fusion.32.code_ref, s32[32,84]{1,0:T(8,128)} %sub.138.run_ref, s32[2]{0:T(128)} %get-tuple-element.257.place_ref, f32[4096,2048]{1,0:T(8,128)} %get-tuple-element.258.front_ref, f32[4096,256]{1,0:T(8,128)} %get-tuple-element.259.rows_ref, ...), custom_call_target="tpu_custom_call" | custom-call | tf_op jit(solution)/shard_map/cond/branch_0_fun/pallas_call | solution.py:415
  517.1 9.6 %branch_0_fun.5 = f32[4096,2048]{1,0:T(8,128)} custom-call(s32[768]{0:T(1024)S(1)} %get-tuple-element.498.block_ref, s32[768]{0:T(1024)S(1)} %get-tuple-element.497.unit_ref, s32[768]{0:T(1024)S(1)} %get-tuple-element.496.index_ref, s32[1]{0:T(128)} %bitcast.count_ref, f32[4096,2048]{1,0:T(8,128)} %branch_0_fun.3.partial_ref, ...), custom_call_target="tpu_custom_call", output_to_operand_aliasing={{}: (4, {})} | custom-call | tf_op jit(solution)/shard_map/cond/branch_0_fun/pallas_call | solution.py:230
  (167 shorter events, 46.2 us)
Async XLA Ops:
  7.4 9.6 %copy-start.20 = (s32[32,128]{1,0:T(8,128)}, s32[32,128]{1,0:T(8,128)S(1)}, u32[]{:S(2)}) copy-start(s32[32,128]{1,0:T(8,128)S(1)} %get-tuple-element.546) | copy-start | bytes 49156
  7.5 13.8 %copy-start.23 = (pred[32,128]{1,0:T(8,128)(4,1)}, pred[32,128]{1,0:T(8,128)(4,1)S(1)}, u32[]{:S(2)}) copy-start(pred[32,128]{1,0:T(8,128)(4,1)S(1)} %get-tuple-element.525) | copy-start | bytes 12292
  17.1 4.1 copy-start.22
  17.2 35.3 %collective-permute-start.8 = (f32[5,128,128]{2,1,0:T(8,128)S(1)}, f32[5,128,128]{2,1,0:T(8,128)S(1)}, u32[]{:S(2)}, u32[]{:S(2)}) collective-permute-start(f32[5,128,128]{2,1,0:T(8,128)S(1)} %get-tuple-element.535), channel_id=1, source_target_pairs={{0,24},{8,0},{16,8},{24,16},{1,25},{9,1},{17,9},{25,17},{2,26},{10... | collective-permute-start | bytes 983048 | tf_op jit(solution)/shard_map/ppermute | solution.py:492
  20.6 31.9 %collective-permute-start.7 = (f32[5,128,128]{2,1,0:T(8,128)S(1)}, f32[5,128,128]{2,1,0:T(8,128)S(1)}, u32[]{:S(2)}, u32[]{:S(2)}) collective-permute-start(f32[5,128,128]{2,1,0:T(8,128)S(1)} %get-tuple-element.536), channel_id=1, source_target_pairs={{0,16},{8,24},{16,0},{24,8},{1,17},{9,25},{17,1},{25,9},{2,18},{10... | collective-permute-start | bytes 983048 | tf_op jit(solution)/shard_map/ppermute | solution.py:492
  20.6 31.9 %collective-permute-start.6 = (f32[5,128,128]{2,1,0:T(8,128)S(1)}, f32[5,128,128]{2,1,0:T(8,128)S(1)}, u32[]{:S(2)}, u32[]{:S(2)}) collective-permute-start(f32[5,128,128]{2,1,0:T(8,128)S(1)} %get-tuple-element.537), channel_id=1, source_target_pairs={{0,8},{8,16},{16,24},{24,0},{1,9},{9,17},{17,25},{25,1},{2,10},{10... | collective-permute-start | bytes 983048 | tf_op jit(solution)/shard_map/ppermute | solution.py:492
  22.4 4.5 copy-start.18
  48.2 4.3 copy-start.4
  55.6 1.9 copy-start.1
  57.5 13.5 %all-to-all-start.2 = ((s32[32,1,84]{2,1,0:T(1,128)}), s32[32,1,84]{2,1,0:T(1,128)S(1)}, u32[]{:S(2)}, u32[]{:S(2)}) async-start(s32[32,1,84]{2,1,0:T(1,128)} %bitcast.46), calls=%async_computation.2 | async-start | bytes 32768 | tf_op jit(solution)/shard_map/all_to_all | solution.py:555
  63.9 24.7 %collective-permute-start.10 = (f32[256,256]{1,0:T(8,128)S(1)}, f32[256,256]{1,0:T(8,128)S(1)}, u32[]{:S(2)}, u32[]{:S(2)}) collective-permute-start(f32[256,256]{1,0:T(8,128)S(1)} %slice_select_fusion.1), channel_id=1, source_target_pairs={{0,16},{1,17},{2,18},{3,19},{4,20},{5,21},{6,22},{7,23}} | collective-permute-start | bytes 786440 | tf_op jit(solution)/shard_map/ppermute | solution.py:508
  68.0 20.7 %collective-permute-start.11 = (f32[256,256]{1,0:T(8,128)S(1)}, f32[256,256]{1,0:T(8,128)S(1)}, u32[]{:S(2)}, u32[]{:S(2)}) collective-permute-start(f32[256,256]{1,0:T(8,128)S(1)} %slice_select_fusion.1), channel_id=1, source_target_pairs={{0,24},{1,25},{2,26},{3,27},{4,28},{5,29},{6,30},{7,31}} | collective-permute-start | bytes 786440 | tf_op jit(solution)/shard_map/ppermute | solution.py:508
  69.6 19.1 %collective-permute-start.9 = (f32[256,256]{1,0:T(8,128)S(1)}, f32[256,256]{1,0:T(8,128)S(1)}, u32[]{:S(2)}, u32[]{:S(2)}) collective-permute-start(f32[256,256]{1,0:T(8,128)S(1)} %slice_select_fusion.1), channel_id=1, source_target_pairs={{0,8},{1,9},{2,10},{3,11},{4,12},{5,13},{6,14},{7,15}} | collective-permute-start | bytes 786440 | tf_op jit(solution)/shard_map/ppermute | solution.py:508
  85.4 8.0 %all-to-all-start.3 = ((s32[32,1,49]{2,1,0:T(1,128)}), s32[32,1,49]{2,1,0:T(1,128)S(1)}, u32[]{:S(2)}, u32[]{:S(2)}) async-start(s32[32,1,49]{2,1,0:T(1,128)} %bitcast.52), calls=%async_computation.3 | async-start | bytes 32768 | tf_op jit(solution)/shard_map/all_to_all | solution.py:582
  93.4 340.3 %all-to-all-start.4 = ((f32[32,84,8,128]{3,2,1,0:T(8,128)}), f32[32,84,8,128]{3,2,1,0:T(8,128)}, u32[]{:S(2)}, u32[]{:S(2)}) async-start(f32[32,84,8,128]{3,2,1,0:T(8,128)} %copy-done.4), calls=%async_computation.4 | async-start | bytes 22020096 | tf_op jit(solution)/shard_map/all_to_all | solution.py:604
  99.4 213.8 %all-reduce.17.cloned.1.call-start = ((), (), s32[]{:S(2)}) async-start(), calls=%async_computation.8 | async-start | bytes 8912896 | tf_op jit(solution)/shard_map/psum | solution.py:603
  100.9 327.0 %all-reduce.15.cloned.1.call-start = ((), (), s32[]{:S(2)}) async-start(), calls=%async_computation.7 | async-start | bytes 4194304 | tf_op jit(solution)/shard_map/psum | solution.py:610
  338.1 3.4 copy-start.15
  366.5 2.2 copy-start.5
  427.9 1.6 copy-start.10
  440.1 9.0 %copy-start.16 = (s32[32,84]{1,0:T(8,128)}, s32[32,84]{1,0:T(8,128)S(1)}, u32[]{:S(2)}) copy-start(s32[32,84]{1,0:T(8,128)S(1)} %get-tuple-element.243) | copy-start | bytes 32260 | tf_op jit(solution)/shard_map/cond
  449.2 1.8 copy-start.3
  451.0 66.1 %all-to-all-start = ((f32[16,48,8,128]{3,2,1,0:T(8,128)}), f32[16,48,8,128]{3,2,1,0:T(8,128)S(1)}, u32[]{:S(2)}, u32[]{:S(2)}) async-start(f32[16,48,8,128]{3,2,1,0:T(8,128)} %bitcast.160), calls=%async_computation | async-start | bytes 6291456 | tf_op jit(solution)/shard_map/cond/branch_0_fun/all_to_all | solution.py:620
  456.4 8.7 %copy-start.17 = (s32[32,84]{1,0:T(8,128)S(1)}, s32[32,84]{1,0:T(8,128)}, u32[]{:S(2)}) copy-start(s32[32,84]{1,0:T(8,128)} %copy-done.16) | copy-start | bytes 32260 | tf_op jit(solution)/shard_map/cond
  466.5 49.3 %copy-start.13 = (s32[768,768]{1,0:T(8,128)S(1)}, s32[768,768]{1,0:T(8,128)}, u32[]{:S(2)}) copy-start(s32[768,768]{1,0:T(8,128)} %get-tuple-element.239) | copy-start | bytes 7077892 | tf_op jit(solution)/shard_map/cond
  466.5 49.3 %copy-start.21 = (s32[768]{0:T(1024)S(1)}, s32[768]{0:T(1024)}, u32[]{:S(2)}) copy-start(s32[768]{0:T(1024)} %reduce_sum.148) | copy-start | bytes 9220 | tf_op jit(solution)/shard_map/cond
Sparse Core Ops, SparseCore 0:
  104.0 209.1 all-reduce.16
  341.3 86.5 all-reduce.14
